TPU v7x, 256 devices: a whole 4x4x8 slice. The times are simulated.
256 devices in a mesh: group: 32 (over x_lo, z, core), inner: 8 (over y, x_hi).
Axes of the slice: x: 4 (x_hi: 2, x_lo: 2; x = x_hi * 2 + x_lo), y: 4, z: 8, core: 2. Of those that a mesh axis runs over, the one named last changes fastest.
Arguments:
- image_emb: bfloat16 [32768, 576], P(('group', 'inner')), may hold values from -8 to 8
- text_feat: bfloat16 [32768, 576], P(('group', 'inner')), may hold values from -8 to 8
- text_head: bfloat16 [576, 576], replicated, may hold values from -1 to 2
- pair_ids: int32 [32768], replicated, may hold values from 0 to 229375, as said below
- logit_scale: float32 [1], replicated, may hold values from 10 to 20
- logit_bias: float32 [1], replicated, may hold values from -8 to -4
Outputs:
- row_loss: float32 [32768], P(('group', 'inner'))
- image_grad: float32 [32768, 576], P(('group', 'inner'))
- text_grad: float32 [32768, 576], P(('group', 'inner'))
- head_grad: float32 [576, 576], replicated
Inputs may be any that keep to these rules, and one draw needn't show every extreme that they name: `pair_ids`: an image and a text match exactly where their ids are equal; every image matches its own text.
All inputs are finite; a program needn't handle non-finite values.
Results may differ from a plain program's by a relative error of at most 0.00115.
The roundings to bfloat16 on the way count: a program that leaves them out, or rounds other values in their place, can miss the bound.
Values may be sent and summed in bfloat16 or wider, within the bound.
A program may use at most 128 MiB of HBM per device.

v0:
```python
import jax
import jax.numpy as jnp
from jax import lax
from jax.sharding import PartitionSpec as P

head_weight_scale = 16.0


def passed_along(value, axis, by):
    peers = lax.axis_size(axis)
    return lax.ppermute(value, axis, [(i, (i + by) % peers) for i in range(peers)])


def normalize(values):
    values_f = values.astype(jnp.float32)
    inv_norm = lax.rsqrt(jnp.sum(values_f * values_f, axis=1, keepdims=True) + 1e-06)
    return (values_f * inv_norm, inv_norm)


def normalize_back(upstream, unit_vals, inv_norm):
    return inv_norm * (upstream - unit_vals * jnp.sum(unit_vals * upstream, axis=1, keepdims=True))


def rotate(text_block):
    return passed_along(text_block, "group", 1)


def shards(image_emb, text_feat, text_head, pair_ids, logit_scale, logit_bias):
    row_count = image_emb.shape[0]
    feature_count = image_emb.shape[1]
    pair_count = pair_ids.shape[0]
    group_count = lax.axis_size("group")
    inner_count = lax.axis_size("inner")
    group_index = lax.axis_index("group")
    inner_index = lax.axis_index("inner")
    logit_mult = logit_scale[0]
    logit_shift = logit_bias[0]
    img_unit_f, img_inv = normalize(image_emb)
    images = lax.all_gather(img_unit_f.astype(jnp.bfloat16), "inner", axis=0, tiled=True)
    image_span = inner_count * row_count
    image_ids = lax.dynamic_slice_in_dim(pair_ids, group_index * image_span, image_span)
    proj = jnp.dot(text_feat, text_head, preferred_element_type=jnp.float32)
    txt_unit_f, txt_inv = normalize(proj)
    txt_unit = txt_unit_f.astype(jnp.bfloat16)

    def score_tile(text_block, owner_group):
        start = (owner_group * inner_count + inner_index) * row_count
        block_ids = lax.dynamic_slice_in_dim(pair_ids, start, row_count)
        logits = (
            logit_mult
            * lax.dot_general(
                text_block, images, (((1,), (1,)), ((), ())), preferred_element_type=jnp.float32
            )
            + logit_shift
        )
        label_sign = jnp.where(block_ids[:, None] == image_ids[None, :], 1.0, -1.0)
        margin = -label_sign * logits
        loss_part = jnp.sum(jax.nn.softplus(margin), axis=0)
        coefficient = (-label_sign * jax.nn.sigmoid(margin)).astype(jnp.bfloat16)
        img_part = logit_mult * lax.dot_general(
            coefficient, text_block, (((0,), (0,)), ((), ())), preferred_element_type=jnp.float32
        )
        txt_part = logit_mult * jnp.dot(coefficient, images, preferred_element_type=jnp.float32)
        return (loss_part, img_part, txt_part)

    loss_init = jnp.zeros((image_span,), jnp.float32)
    image_init = jnp.zeros((image_span, feature_count), jnp.float32)

    def advance(carry_state, step_index):
        text_block, carried, loss_total, image_total = carry_state
        owner_group = (group_index - step_index) % group_count
        loss_part, img_part, txt_part = score_tile(text_block, owner_group)
        carried = passed_along(carried + txt_part, "group", 1)
        return (rotate(text_block), carried, loss_total + loss_part, image_total + img_part)

    def two_steps(turn_index, carry_state):
        carry_state = advance(carry_state, 2 * turn_index)
        return advance(carry_state, 2 * turn_index + 1)

    start_state = (
        txt_unit,
        jnp.zeros((row_count, feature_count), jnp.float32),
        loss_init,
        image_init,
    )
    final_state = lax.fori_loop(0, group_count // 2, two_steps, start_state)
    txt_unit_grad = final_state[1]
    loss_total = final_state[2]
    image_total = final_state[3]
    img_unit_grad, loss_rows = (
        lax.psum_scatter(image_total, "inner", scatter_dimension=0, tiled=True),
        lax.psum_scatter(loss_total, "inner", scatter_dimension=0, tiled=True),
    )
    row_loss = loss_rows / pair_count
    image_grad = normalize_back(img_unit_grad, img_unit_f, img_inv)
    proj_grad = normalize_back(txt_unit_grad, txt_unit_f, txt_inv).astype(jnp.bfloat16)
    text_grad = lax.dot_general(
        proj_grad, text_head, (((1,), (1,)), ((), ())), preferred_element_type=jnp.float32
    )
    head_part = head_weight_scale * lax.dot_general(
        text_feat, proj_grad, (((0,), (0,)), ((), ())), preferred_element_type=jnp.float32
    )
    head_grad = lax.psum(head_part, ("group", "inner"))
    return (row_loss, image_grad, text_grad, head_grad)


def solution(mesh):
    return jax.shard_map(
        shards,
        mesh=mesh,
        in_specs=(P(("group", "inner"), None), P(("group", "inner"), None), P(), P(), P(), P()),
        out_specs=(
            P(("group", "inner")),
            P(("group", "inner"), None),
            P(("group", "inner"), None),
            P(),
        ),
        check_vma=False,
    )
```

profile of v0, /device:TPU:1, one launch (start us, length us, event | category | flops | bytes accessed | tf_op | source)
XLA Modules:
  0.0 877.4 jit_solution(4835678764981566075)
XLA Ops:
  13.4 52.5 %all-gather.2.cloned.1.call-done = bf16[1024,576]{0,1:T(8,128)(2,1)} async-done(((bf16[128,576]{0,1:T(8,128)(2,1)}), bf16[1024,576]{0,1:T(8,128)(2,1)}) %all-gather.2.cloned.1.call-update) | async-done | bytes 1179664 | tf_op jit(solution)/shard_map/all_gather | solution.py:39
  69.0 453.2 %while.22 = (s32[]{:T(128)}, bf16[128,576]{1,0:T(8,128)(2,1)S(1)}, f32[128,576]{0,1:T(8,128)}, f32[1024]{0:T(1024)}, f32[1024,576]{0,1:T(8,128)}, /*index=5*/f32...) while((s32[]{:T(128)}, bf16[128,576]{1,0:T(8,128)(2,1)S(1)}, ...), condition=%wide.region_5.6_spmd.clone, body=%wide.region_2.5_spmd.clone.sunk | while | flops 916816896 | bytes 41590728 | solution.py:86
  72.6 4.0 fusion.59
  83.1 3.4 fusion.61
  97.2 4.0 fusion.59
  108.4 3.4 fusion.61
  122.5 4.0 fusion.59
  126.5 3.4 fusion.60
  135.3 3.4 fusion.61
  144.6 4.4 collective-permute-done.3
  150.5 4.0 fusion.59
  154.5 3.4 fusion.60
  162.2 3.4 fusion.61
  172.2 5.5 collective-permute-done.3
  179.2 4.0 fusion.59
  189.1 3.4 fusion.61
  200.9 5.5 collective-permute-done.3
  207.9 4.0 fusion.59
  216.7 3.4 fusion.61
  220.2 3.7 collective-permute-done.2
  229.6 5.5 collective-permute-done.3
  236.6 4.0 fusion.59
  245.4 3.4 fusion.61
  248.9 3.7 collective-permute-done.2
  258.4 5.5 collective-permute-done.3
  265.3 4.0 fusion.59
  274.1 3.4 fusion.61
  277.6 3.7 collective-permute-done.2
  287.1 5.5 collective-permute-done.3
  294.0 4.0 fusion.59
  302.8 3.4 fusion.61
  306.3 3.7 collective-permute-done.2
  315.8 5.5 collective-permute-done.3
  322.7 4.0 fusion.59
  331.5 3.4 fusion.61
  335.0 3.7 collective-permute-done.2
  344.5 5.5 collective-permute-done.3
  351.4 4.0 fusion.59
  360.2 3.4 fusion.61
  363.7 3.7 collective-permute-done.2
  373.2 5.5 collective-permute-done.3
  380.1 4.0 fusion.59
  389.0 3.4 fusion.61
  392.4 3.7 collective-permute-done.2
  401.9 5.5 collective-permute-done.3
  408.8 4.0 fusion.59
  417.7 3.4 fusion.61
  421.1 3.7 collective-permute-done.2
  430.6 5.5 collective-permute-done.3
  437.5 4.0 fusion.59
  446.4 3.4 fusion.61
  449.8 3.7 collective-permute-done.2
  459.3 5.5 collective-permute-done.3
  466.2 4.0 fusion.59
  475.1 3.4 fusion.61
  478.5 3.7 collective-permute-done.2
  488.0 5.5 collective-permute-done.3
  494.9 4.0 fusion.59
  503.8 3.4 fusion.61
  507.2 3.7 collective-permute-done.2
  516.7 5.5 collective-permute-done.3
  528.7 16.7 %all-reduce = f32[1024]{0:T(1024)S(1)} all-reduce(f32[1024]{0:T(1024)S(1)} %copy-done.6), channel_id=2, replica_groups=mesh['group'=32,'inner'=8] {'inner'}, use_global_device_ids=true, to_apply=%region_6.7.clone | all-reduce | flops 1024 | bytes 8192
  547.1 236.4 %all-reduce.3.cloned.1.call-done = f32[576,576]{0,1:T(8,128)} async-done(((f32[576,576]{0,1:T(8,128)}), f32[576,576]{0,1:T(8,128)}) %all-reduce.3.cloned.1.call-update) | async-done | bytes 1327120 | tf_op jit(solution)/shard_map/psum | solution.py:103
  786.4 81.6 %reduce-scatter.2.cloned.1.call-done = f32[128,576]{0,1:T(8,128)} async-done(((f32[1024,576]{0,1:T(8,128)}), f32[128,576]{0,1:T(8,128)}) %reduce-scatter.2.cloned.1.call-update) | async-done | bytes 294928 | tf_op jit(solution)/shard_map/reduce_scatter | solution.py:91
  (430 shorter events, 230.1 us)
Async XLA Ops:
  7.2 58.7 %all-gather.2.cloned.1.call-start = ((), (), s32[]{:S(2)}) async-start(), calls=%async_computation.1 | async-start | bytes 1327104 | tf_op jit(solution)/shard_map/all_gather | solution.py:39
  9.9 773.5 %all-reduce.3.cloned.1.call-start = ((), (), s32[]{:S(2)}) async-start(), calls=%async_computation.3 | async-start | bytes 2949120 | tf_op jit(solution)/shard_map/psum | solution.py:103
  69.0 12.3 %collective-permute-start = (bf16[128,576]{1,0:T(8,128)(2,1)S(1)}, bf16[128,576]{1,0:T(8,128)(2,1)}, u32[]{:S(2)}, u32[]{:S(2)}) collective-permute-start(bf16[128,576]{1,0:T(8,128)(2,1)S(1)} %get-tuple-element.505), channel_id=1, source_target_pairs={{0,8},{8,16},{16,24},{24,32},{32,40},{40,48},{48,56},{56,64},{64,7... | collective-permute-start | bytes 442376 | tf_op jit(solution)/shard_map/while/body/eval_jaxpr/ppermute | solution.py:11
  81.4 11.0 %collective-permute-start.1 = (bf16[128,576]{1,0:T(8,128)(2,1)}, bf16[128,576]{1,0:T(8,128)(2,1)S(1)}, u32[]{:S(2)}, u32[]{:S(2)}) collective-permute-start(bf16[128,576]{1,0:T(8,128)(2,1)} %collective-permute-done), channel_id=1, source_target_pairs={{0,8},{8,16},{16,24},{24,32},{32,40},{40,48},{48,56},{56,64},{64,7... | collective-permute-start | bytes 442376 | tf_op jit(solution)/shard_map/while/body/eval_jaxpr/ppermute | solution.py:11
  93.7 12.2 %collective-permute-start = (bf16[128,576]{1,0:T(8,128)(2,1)S(1)}, bf16[128,576]{1,0:T(8,128)(2,1)}, u32[]{:S(2)}, u32[]{:S(2)}) collective-permute-start(bf16[128,576]{1,0:T(8,128)(2,1)S(1)} %get-tuple-element.505), channel_id=1, source_target_pairs={{0,8},{8,16},{16,24},{24,32},{32,40},{40,48},{48,56},{56,64},{64,7... | collective-permute-start | bytes 442376 | tf_op jit(solution)/shard_map/while/body/eval_jaxpr/ppermute | solution.py:11
  104.6 7.3 collective-permute-start.2
  105.9 11.8 %collective-permute-start.1 = (bf16[128,576]{1,0:T(8,128)(2,1)}, bf16[128,576]{1,0:T(8,128)(2,1)S(1)}, u32[]{:S(2)}, u32[]{:S(2)}) collective-permute-start(bf16[128,576]{1,0:T(8,128)(2,1)} %collective-permute-done), channel_id=1, source_target_pairs={{0,8},{8,16},{16,24},{24,32},{32,40},{40,48},{48,56},{56,64},{64,7... | collective-permute-start | bytes 442376 | tf_op jit(solution)/shard_map/while/body/eval_jaxpr/ppermute | solution.py:11
  120.3 11.6 %collective-permute-start = (bf16[128,576]{1,0:T(8,128)(2,1)S(1)}, bf16[128,576]{1,0:T(8,128)(2,1)}, u32[]{:S(2)}, u32[]{:S(2)}) collective-permute-start(bf16[128,576]{1,0:T(8,128)(2,1)S(1)} %get-tuple-element.505), channel_id=1, source_target_pairs={{0,8},{8,16},{16,24},{24,32},{32,40},{40,48},{48,56},{56,64},{64,7... | collective-permute-start | bytes 442376 | tf_op jit(solution)/shard_map/while/body/eval_jaxpr/ppermute | solution.py:11
  129.9 8.8 %collective-permute-start.2 = (f32[128,576]{0,1:T(8,128)}, f32[128,576]{0,1:T(8,128)}, u32[]{:S(2)}, u32[]{:S(2)}) collective-permute-start(f32[128,576]{0,1:T(8,128)} %fusion.60), channel_id=1, source_target_pairs={{0,8},{8,16},{16,24},{24,32},{32,40},{40,48},{48,56},{56,64},{64,7... | collective-permute-start | bytes 884744 | tf_op jit(solution)/shard_map/while/body/eval_jaxpr/ppermute | solution.py:11
  131.9 12.6 %collective-permute-start.1 = (bf16[128,576]{1,0:T(8,128)(2,1)}, bf16[128,576]{1,0:T(8,128)(2,1)S(1)}, u32[]{:S(2)}, u32[]{:S(2)}) collective-permute-start(bf16[128,576]{1,0:T(8,128)(2,1)} %collective-permute-done), channel_id=1, source_target_pairs={{0,8},{8,16},{16,24},{24,32},{32,40},{40,48},{48,56},{56,64},{64,7... | collective-permute-start | bytes 442376 | tf_op jit(solution)/shard_map/while/body/eval_jaxpr/ppermute | solution.py:11
  141.6 7.4 collective-permute-start.3
  149.0 10.2 %collective-permute-start = (bf16[128,576]{1,0:T(8,128)(2,1)S(1)}, bf16[128,576]{1,0:T(8,128)(2,1)}, u32[]{:S(2)}, u32[]{:S(2)}) collective-permute-start(bf16[128,576]{1,0:T(8,128)(2,1)S(1)} %get-tuple-element.505), channel_id=1, source_target_pairs={{0,8},{8,16},{16,24},{24,32},{32,40},{40,48},{48,56},{56,64},{64,7... | collective-permute-start | bytes 442376 | tf_op jit(solution)/shard_map/while/body/eval_jaxpr/ppermute | solution.py:11
  157.9 8.6 collective-permute-start.2
  159.2 13.0 %collective-permute-start.1 = (bf16[128,576]{1,0:T(8,128)(2,1)}, bf16[128,576]{1,0:T(8,128)(2,1)S(1)}, u32[]{:S(2)}, u32[]{:S(2)}) collective-permute-start(bf16[128,576]{1,0:T(8,128)(2,1)} %collective-permute-done), channel_id=1, source_target_pairs={{0,8},{8,16},{16,24},{24,32},{32,40},{40,48},{48,56},{56,64},{64,7... | collective-permute-start | bytes 442376 | tf_op jit(solution)/shard_map/while/body/eval_jaxpr/ppermute | solution.py:11
  169.3 8.4 collective-permute-start.3
  177.7 10.2 %collective-permute-start = (bf16[128,576]{1,0:T(8,128)(2,1)S(1)}, bf16[128,576]{1,0:T(8,128)(2,1)}, u32[]{:S(2)}, u32[]{:S(2)}) collective-permute-start(bf16[128,576]{1,0:T(8,128)(2,1)S(1)} %get-tuple-element.505), channel_id=1, source_target_pairs={{0,8},{8,16},{16,24},{24,32},{32,40},{40,48},{48,56},{56,64},{64,7... | collective-permute-start | bytes 442376 | tf_op jit(solution)/shard_map/while/body/eval_jaxpr/ppermute | solution.py:11
  186.6 8.6 collective-permute-start.2
  187.9 13.0 %collective-permute-start.1 = (bf16[128,576]{1,0:T(8,128)(2,1)}, bf16[128,576]{1,0:T(8,128)(2,1)S(1)}, u32[]{:S(2)}, u32[]{:S(2)}) collective-permute-start(bf16[128,576]{1,0:T(8,128)(2,1)} %collective-permute-done), channel_id=1, source_target_pairs={{0,8},{8,16},{16,24},{24,32},{32,40},{40,48},{48,56},{56,64},{64,7... | collective-permute-start | bytes 442376 | tf_op jit(solution)/shard_map/while/body/eval_jaxpr/ppermute | solution.py:11
  198.0 8.4 collective-permute-start.3
  206.4 10.2 %collective-permute-start = (bf16[128,576]{1,0:T(8,128)(2,1)S(1)}, bf16[128,576]{1,0:T(8,128)(2,1)}, u32[]{:S(2)}, u32[]{:S(2)}) collective-permute-start(bf16[128,576]{1,0:T(8,128)(2,1)S(1)} %get-tuple-element.505), channel_id=1, source_target_pairs={{0,8},{8,16},{16,24},{24,32},{32,40},{40,48},{48,56},{56,64},{64,7... | collective-permute-start | bytes 442376 | tf_op jit(solution)/shard_map/while/body/eval_jaxpr/ppermute | solution.py:11
  215.3 8.6 collective-permute-start.2
  216.6 13.0 %collective-permute-start.1 = (bf16[128,576]{1,0:T(8,128)(2,1)}, bf16[128,576]{1,0:T(8,128)(2,1)S(1)}, u32[]{:S(2)}, u32[]{:S(2)}) collective-permute-start(bf16[128,576]{1,0:T(8,128)(2,1)} %collective-permute-done), channel_id=1, source_target_pairs={{0,8},{8,16},{16,24},{24,32},{32,40},{40,48},{48,56},{56,64},{64,7... | collective-permute-start | bytes 442376 | tf_op jit(solution)/shard_map/while/body/eval_jaxpr/ppermute | solution.py:11
  226.7 8.4 collective-permute-start.3
  235.1 10.2 %collective-permute-start = (bf16[128,576]{1,0:T(8,128)(2,1)S(1)}, bf16[128,576]{1,0:T(8,128)(2,1)}, u32[]{:S(2)}, u32[]{:S(2)}) collective-permute-start(bf16[128,576]{1,0:T(8,128)(2,1)S(1)} %get-tuple-element.505), channel_id=1, source_target_pairs={{0,8},{8,16},{16,24},{24,32},{32,40},{40,48},{48,56},{56,64},{64,7... | collective-permute-start | bytes 442376 | tf_op jit(solution)/shard_map/while/body/eval_jaxpr/ppermute | solution.py:11
  244.0 8.6 collective-permute-start.2
  245.3 13.0 %collective-permute-start.1 = (bf16[128,576]{1,0:T(8,128)(2,1)}, bf16[128,576]{1,0:T(8,128)(2,1)S(1)}, u32[]{:S(2)}, u32[]{:S(2)}) collective-permute-start(bf16[128,576]{1,0:T(8,128)(2,1)} %collective-permute-done), channel_id=1, source_target_pairs={{0,8},{8,16},{16,24},{24,32},{32,40},{40,48},{48,56},{56,64},{64,7... | collective-permute-start | bytes 442376 | tf_op jit(solution)/shard_map/while/body/eval_jaxpr/ppermute | solution.py:11
  255.4 8.4 collective-permute-start.3
  263.9 10.2 %collective-permute-start = (bf16[128,576]{1,0:T(8,128)(2,1)S(1)}, bf16[128,576]{1,0:T(8,128)(2,1)}, u32[]{:S(2)}, u32[]{:S(2)}) collective-permute-start(bf16[128,576]{1,0:T(8,128)(2,1)S(1)} %get-tuple-element.505), channel_id=1, source_target_pairs={{0,8},{8,16},{16,24},{24,32},{32,40},{40,48},{48,56},{56,64},{64,7... | collective-permute-start | bytes 442376 | tf_op jit(solution)/shard_map/while/body/eval_jaxpr/ppermute | solution.py:11
  272.7 8.6 collective-permute-start.2
  274.0 13.0 %collective-permute-start.1 = (bf16[128,576]{1,0:T(8,128)(2,1)}, bf16[128,576]{1,0:T(8,128)(2,1)S(1)}, u32[]{:S(2)}, u32[]{:S(2)}) collective-permute-start(bf16[128,576]{1,0:T(8,128)(2,1)} %collective-permute-done), channel_id=1, source_target_pairs={{0,8},{8,16},{16,24},{24,32},{32,40},{40,48},{48,56},{56,64},{64,7... | collective-permute-start | bytes 442376 | tf_op jit(solution)/shard_map/while/body/eval_jaxpr/ppermute | solution.py:11
  284.1 8.4 collective-permute-start.3
  292.6 10.2 %collective-permute-start = (bf16[128,576]{1,0:T(8,128)(2,1)S(1)}, bf16[128,576]{1,0:T(8,128)(2,1)}, u32[]{:S(2)}, u32[]{:S(2)}) collective-permute-start(bf16[128,576]{1,0:T(8,128)(2,1)S(1)} %get-tuple-element.505), channel_id=1, source_target_pairs={{0,8},{8,16},{16,24},{24,32},{32,40},{40,48},{48,56},{56,64},{64,7... | collective-permute-start | bytes 442376 | tf_op jit(solution)/shard_map/while/body/eval_jaxpr/ppermute | solution.py:11
  301.4 8.6 collective-permute-start.2
  302.7 13.0 %collective-permute-start.1 = (bf16[128,576]{1,0:T(8,128)(2,1)}, bf16[128,576]{1,0:T(8,128)(2,1)S(1)}, u32[]{:S(2)}, u32[]{:S(2)}) collective-permute-start(bf16[128,576]{1,0:T(8,128)(2,1)} %collective-permute-done), channel_id=1, source_target_pairs={{0,8},{8,16},{16,24},{24,32},{32,40},{40,48},{48,56},{56,64},{64,7... | collective-permute-start | bytes 442376 | tf_op jit(solution)/shard_map/while/body/eval_jaxpr/ppermute | solution.py:11
  312.8 8.4 collective-permute-start.3
  321.3 10.2 %collective-permute-start = (bf16[128,576]{1,0:T(8,128)(2,1)S(1)}, bf16[128,576]{1,0:T(8,128)(2,1)}, u32[]{:S(2)}, u32[]{:S(2)}) collective-permute-start(bf16[128,576]{1,0:T(8,128)(2,1)S(1)} %get-tuple-element.505), channel_id=1, source_target_pairs={{0,8},{8,16},{16,24},{24,32},{32,40},{40,48},{48,56},{56,64},{64,7... | collective-permute-start | bytes 442376 | tf_op jit(solution)/shard_map/while/body/eval_jaxpr/ppermute | solution.py:11
  330.1 8.6 collective-permute-start.2
  331.4 13.0 %collective-permute-start.1 = (bf16[128,576]{1,0:T(8,128)(2,1)}, bf16[128,576]{1,0:T(8,128)(2,1)S(1)}, u32[]{:S(2)}, u32[]{:S(2)}) collective-permute-start(bf16[128,576]{1,0:T(8,128)(2,1)} %collective-permute-done), channel_id=1, source_target_pairs={{0,8},{8,16},{16,24},{24,32},{32,40},{40,48},{48,56},{56,64},{64,7... | collective-permute-start | bytes 442376 | tf_op jit(solution)/shard_map/while/body/eval_jaxpr/ppermute | solution.py:11
  341.5 8.4 collective-permute-start.3
  350.0 10.2 %collective-permute-start = (bf16[128,576]{1,0:T(8,128)(2,1)S(1)}, bf16[128,576]{1,0:T(8,128)(2,1)}, u32[]{:S(2)}, u32[]{:S(2)}) collective-permute-start(bf16[128,576]{1,0:T(8,128)(2,1)S(1)} %get-tuple-element.505), channel_id=1, source_target_pairs={{0,8},{8,16},{16,24},{24,32},{32,40},{40,48},{48,56},{56,64},{64,7... | collective-permute-start | bytes 442376 | tf_op jit(solution)/shard_map/while/body/eval_jaxpr/ppermute | solution.py:11
  358.8 8.6 collective-permute-start.2
  360.1 13.0 %collective-permute-start.1 = (bf16[128,576]{1,0:T(8,128)(2,1)}, bf16[128,576]{1,0:T(8,128)(2,1)S(1)}, u32[]{:S(2)}, u32[]{:S(2)}) collective-permute-start(bf16[128,576]{1,0:T(8,128)(2,1)} %collective-permute-done), channel_id=1, source_target_pairs={{0,8},{8,16},{16,24},{24,32},{32,40},{40,48},{48,56},{56,64},{64,7... | collective-permute-start | bytes 442376 | tf_op jit(solution)/shard_map/while/body/eval_jaxpr/ppermute | solution.py:11
  370.2 8.4 collective-permute-start.3
  378.7 10.2 %collective-permute-start = (bf16[128,576]{1,0:T(8,128)(2,1)S(1)}, bf16[128,576]{1,0:T(8,128)(2,1)}, u32[]{:S(2)}, u32[]{:S(2)}) collective-permute-start(bf16[128,576]{1,0:T(8,128)(2,1)S(1)} %get-tuple-element.505), channel_id=1, source_target_pairs={{0,8},{8,16},{16,24},{24,32},{32,40},{40,48},{48,56},{56,64},{64,7... | collective-permute-start | bytes 442376 | tf_op jit(solution)/shard_map/while/body/eval_jaxpr/ppermute | solution.py:11
  387.5 8.6 collective-permute-start.2
  388.9 13.0 %collective-permute-start.1 = (bf16[128,576]{1,0:T(8,128)(2,1)}, bf16[128,576]{1,0:T(8,128)(2,1)S(1)}, u32[]{:S(2)}, u32[]{:S(2)}) collective-permute-start(bf16[128,576]{1,0:T(8,128)(2,1)} %collective-permute-done), channel_id=1, source_target_pairs={{0,8},{8,16},{16,24},{24,32},{32,40},{40,48},{48,56},{56,64},{64,7... | collective-permute-start | bytes 442376 | tf_op jit(solution)/shard_map/while/body/eval_jaxpr/ppermute | solution.py:11
  398.9 8.4 collective-permute-start.3
  407.4 10.2 %collective-permute-start = (bf16[128,576]{1,0:T(8,128)(2,1)S(1)}, bf16[128,576]{1,0:T(8,128)(2,1)}, u32[]{:S(2)}, u32[]{:S(2)}) collective-permute-start(bf16[128,576]{1,0:T(8,128)(2,1)S(1)} %get-tuple-element.505), channel_id=1, source_target_pairs={{0,8},{8,16},{16,24},{24,32},{32,40},{40,48},{48,56},{56,64},{64,7... | collective-permute-start | bytes 442376 | tf_op jit(solution)/shard_map/while/body/eval_jaxpr/ppermute | solution.py:11
  416.2 8.6 collective-permute-start.2
  417.6 13.0 %collective-permute-start.1 = (bf16[128,576]{1,0:T(8,128)(2,1)}, bf16[128,576]{1,0:T(8,128)(2,1)S(1)}, u32[]{:S(2)}, u32[]{:S(2)}) collective-permute-start(bf16[128,576]{1,0:T(8,128)(2,1)} %collective-permute-done), channel_id=1, source_target_pairs={{0,8},{8,16},{16,24},{24,32},{32,40},{40,48},{48,56},{56,64},{64,7... | collective-permute-start | bytes 442376 | tf_op jit(solution)/shard_map/while/body/eval_jaxpr/ppermute | solution.py:11
  427.6 8.4 collective-permute-start.3
  436.1 10.2 %collective-permute-start = (bf16[128,576]{1,0:T(8,128)(2,1)S(1)}, bf16[128,576]{1,0:T(8,128)(2,1)}, u32[]{:S(2)}, u32[]{:S(2)}) collective-permute-start(bf16[128,576]{1,0:T(8,128)(2,1)S(1)} %get-tuple-element.505), channel_id=1, source_target_pairs={{0,8},{8,16},{16,24},{24,32},{32,40},{40,48},{48,56},{56,64},{64,7... | collective-permute-start | bytes 442376 | tf_op jit(solution)/shard_map/while/body/eval_jaxpr/ppermute | solution.py:11
  444.9 8.6 collective-permute-start.2
  446.3 13.0 %collective-permute-start.1 = (bf16[128,576]{1,0:T(8,128)(2,1)}, bf16[128,576]{1,0:T(8,128)(2,1)S(1)}, u32[]{:S(2)}, u32[]{:S(2)}) collective-permute-start(bf16[128,576]{1,0:T(8,128)(2,1)} %collective-permute-done), channel_id=1, source_target_pairs={{0,8},{8,16},{16,24},{24,32},{32,40},{40,48},{48,56},{56,64},{64,7... | collective-permute-start | bytes 442376 | tf_op jit(solution)/shard_map/while/body/eval_jaxpr/ppermute | solution.py:11
  456.4 8.4 collective-permute-start.3
  464.8 10.2 %collective-permute-start = (bf16[128,576]{1,0:T(8,128)(2,1)S(1)}, bf16[128,576]{1,0:T(8,128)(2,1)}, u32[]{:S(2)}, u32[]{:S(2)}) collective-permute-start(bf16[128,576]{1,0:T(8,128)(2,1)S(1)} %get-tuple-element.505), channel_id=1, source_target_pairs={{0,8},{8,16},{16,24},{24,32},{32,40},{40,48},{48,56},{56,64},{64,7... | collective-permute-start | bytes 442376 | tf_op jit(solution)/shard_map/while/body/eval_jaxpr/ppermute | solution.py:11
  473.7 8.6 collective-permute-start.2
  475.0 13.0 %collective-permute-start.1 = (bf16[128,576]{1,0:T(8,128)(2,1)}, bf16[128,576]{1,0:T(8,128)(2,1)S(1)}, u32[]{:S(2)}, u32[]{:S(2)}) collective-permute-start(bf16[128,576]{1,0:T(8,128)(2,1)} %collective-permute-done), channel_id=1, source_target_pairs={{0,8},{8,16},{16,24},{24,32},{32,40},{40,48},{48,56},{56,64},{64,7... | collective-permute-start | bytes 442376 | tf_op jit(solution)/shard_map/while/body/eval_jaxpr/ppermute | solution.py:11
  485.1 8.4 collective-permute-start.3
  493.5 10.2 %collective-permute-start = (bf16[128,576]{1,0:T(8,128)(2,1)S(1)}, bf16[128,576]{1,0:T(8,128)(2,1)}, u32[]{:S(2)}, u32[]{:S(2)}) collective-permute-start(bf16[128,576]{1,0:T(8,128)(2,1)S(1)} %get-tuple-element.505), channel_id=1, source_target_pairs={{0,8},{8,16},{16,24},{24,32},{32,40},{40,48},{48,56},{56,64},{64,7... | collective-permute-start | bytes 442376 | tf_op jit(solution)/shard_map/while/body/eval_jaxpr/ppermute | solution.py:11
  502.4 8.6 collective-permute-start.2
  503.7 13.0 %collective-permute-start.1 = (bf16[128,576]{1,0:T(8,128)(2,1)}, bf16[128,576]{1,0:T(8,128)(2,1)S(1)}, u32[]{:S(2)}, u32[]{:S(2)}) collective-permute-start(bf16[128,576]{1,0:T(8,128)(2,1)} %collective-permute-done), channel_id=1, source_target_pairs={{0,8},{8,16},{16,24},{24,32},{32,40},{40,48},{48,56},{56,64},{64,7... | collective-permute-start | bytes 442376 | tf_op jit(solution)/shard_map/while/body/eval_jaxpr/ppermute | solution.py:11
  513.8 8.4 collective-permute-start.3
  526.7 341.4 %reduce-scatter.2.cloned.1.call-start = ((), (), s32[]{:S(2)}) async-start(), calls=%async_computation.2 | async-start | bytes 2654208 | tf_op jit(solution)/shard_map/reduce_scatter | solution.py:91
  (106 other events, 1062.7 us)
Sparse Core Ops, SparseCore 0:
  11.1 54.7 all-gather.1
  526.8 256.6 all-reduce.2
  788.1 79.9 reduce-scatter.1
where the time goes:
time: 882 us; the launch traced here: 877 us
  waiting for transfers between devices  495 us (56%)
  matrix products  289 us (33%)
  local copies, waits for them, and re-layouts  31.6 us (4%)
  starting transfers between devices  20.2 us (2%)
  blocking collectives  16.7 us (2%)
  between operations  14.5 us (2%)
    psum x1, waiting for transfers between devices, shards(): head_grad = lax.psum(head_part, ('group', 'inner'))  236 us
    ppermute x64, waiting for transfers between devices, passed_along(): lax.ppermute(value, axis, [(i, (i + by) % peers) for i in range(peers)])  123 us
    dot_general x32, matrix products, score_tile(): lax.dot_general(text_block, images, (((1,), (1,)), ((), ())), preferred_e...  119 us
    dot_general x32, matrix products, score_tile(): jnp.dot(coefficient, images, preferred_element_type=jnp.float32)  99.5 us
    reduce_scatter x1, waiting for transfers between devices, shards(): lax.psum_scatter(image_total, 'inner', scatter_dimension=0, tiled=True)  81.6 us
    dot_general x32, matrix products, score_tile(): lax.dot_general(coefficient, text_block, (((0,), (0,)), ((), ())), prefer...  64.8 us
    all_gather x1, waiting for transfers between devices, shards(): lax.all_gather(img_unit_f.astype(jnp.bfloat16), 'inner', axis=0, tiled=True)  52.5 us
    dynamic_slice x16, local copies, waits for them, and re-layouts, score_tile(): block_ids = lax.dynamic_slice_in_dim(pair_ids, start, row_count)  22 us
  transfers between devices with their start and end apart: 67, of which 32 were waited for; matrix products, arithmetic and copies ran while one was open for 36% of the time, Pallas kernels for 0%

commit v1 on v0

v1 whole, which is shorter than its diff:
```python
import functools
import jax
import jax.numpy as jnp
from jax import lax
from jax.experimental import pallas as pl
from jax.experimental.pallas import tpu as pltpu
from jax.sharding import PartitionSpec as P

HEAD_SCALE = 16.0
LOG2E = 1.4426950408889634
D = 576
B = 128
GR = D + 8
HT = 384
f32 = jnp.float32
bf16 = jnp.bfloat16


def dg(a, b, ca, cb):
    return lax.dot_general(a, b, (((ca,), (cb,)), ((), ())), preferred_element_type=f32)


def coords():
    g = lax.axis_index("group")
    i = lax.axis_index("inner")
    return lax.rem(i, 2) * 2 + g // 16, i // 2, lax.rem(g // 2, 8), lax.rem(g, 2)


def mesh_id(x, y, z, c):
    return (lax.rem(x, 2) * 8 + z) * 2 + c, y * 2 + x // 2


def peer(kp=0, kq=0, kz=0, kc=0):
    x, y, z, c = coords()
    dx = jnp.where(c == 0, kp, kq)
    dy = jnp.where(c == 0, kq, kp)
    return mesh_id(
        lax.rem(x + dx + 4, 4), lax.rem(y + dy + 4, 4), lax.rem(z + kz + 8, 8), lax.rem(c + kc, 2)
    )


def remote(src, dst, ss, rs, **k):
    return pltpu.make_async_remote_copy(
        src_ref=src, dst_ref=dst, send_sem=ss, recv_sem=rs,
        device_id=peer(**k), device_id_type=pl.DeviceIdType.MESH,
    )


def unit_rows(v):
    inv = lax.rsqrt(jnp.sum(v * v, axis=1, keepdims=True) + 1e-06)
    return v * inv, inv


def normalize_back(up, unit, inv):
    return inv * (up - unit * jnp.sum(unit * up, axis=1, keepdims=True))


def score(dots, match, s2, b2):
    z = dots * s2 + b2
    m = jnp.where(match, -z, z)
    u = jnp.exp2(m)
    w = 1.0 + u
    r = 1.0 / w
    sg = u * r
    loss = jnp.log(w) + (u - (w - 1.0)) * r
    return loss, jnp.where(match, -sg, sg).astype(bf16)


def kernel(scale_ref, bias_ref, emb, feat, head, ids,
           loss_out, img_out, txt_out, head_out,
           imgT, img, txtT, idi, lacc, gi, gt, imgu, txtu, invs,
           rcore, rright, rleft, r1, r2, hp, hcore, hP, hQ, hz, res,
           s_ag, r_ag, s_rs, r_rs, s_ar, r_ar):
    x, y, z, c = coords()
    pp = jnp.where(c == 0, x, y)
    qq = jnp.where(c == 0, y, x)
    bar = pltpu.get_barrier_semaphore()
    partners = ([dict(kp=k) for k in (1, 2, 3)] + [dict(kq=k) for k in (1, 2, 3)]
                + [dict(kz=k) for k in range(1, 8)] + [dict(kc=1)])
    for k in partners:
        pl.semaphore_signal(bar, inc=1, device_id=peer(**k), device_id_type=pl.DeviceIdType.MESH)

    u, inv = unit_rows(emb[...].astype(f32))
    imgu[...] = u
    invs[0] = inv * jnp.ones((1, B), f32)
    imgT[0] = u.T.astype(bf16)
    v, vinv = unit_rows(jnp.dot(feat[...], head[...], preferred_element_type=f32))
    txtu[...] = v
    invs[1] = vinv * jnp.ones((1, B), f32)
    txtT[0, 0] = v.T.astype(bf16)
    pl.semaphore_wait(bar, len(partners))

    n = [0]

    def ag(src, dst, **k):
        j = n[0]
        n[0] += 1
        return remote(src, dst, s_ag.at[j], r_ag.at[j], **k)

    started = []

    def go(cp):
        cp.start()
        started.append(cp)
        return cp

    p_in = {k: go(ag(imgT.at[0], imgT.at[k], kp=k)) for k in (1, 3, 2)}
    right = go(ag(txtT.at[0, 0], txtT.at[7, 0], kz=1))
    left = go(ag(txtT.at[0, 0], txtT.at[1, 0], kz=-1))
    sib = [go(ag(txtT.at[0, 0], txtT.at[0, 1], kc=1))]
    q_in = [go(ag(imgT.at[0], imgT.at[4 * k], kq=k)) for k in (1, 3, 2)]

    gi[...] = jnp.zeros_like(gi)
    lacc[...] = jnp.zeros_like(lacc)

    def p_forward(j):
        p_in[j].wait_recv()
        for k in (1, 3, 2):
            q_in.append(go(ag(imgT.at[j], imgT.at[4 * k + j], kq=k)))

    def z_forward(s):
        nonlocal right, left
        right.wait_recv()
        a = 7 - s
        if s < 3:
            nxt = go(ag(txtT.at[a, 0], txtT.at[a - 1, 0], kz=1))
        sib.append(go(ag(txtT.at[a, 0], txtT.at[a, 1], kc=1)))
        if s < 3:
            right = nxt
            left.wait_recv()
            b = 1 + s
            if s < 2:
                left = go(ag(txtT.at[b, 0], txtT.at[b + 1, 0], kz=-1))
            sib.append(go(ag(txtT.at[b, 0], txtT.at[b, 1], kc=1)))

    p_forward(1)
    p_forward(3)
    z_forward(0)
    p_forward(2)
    z_forward(1)
    z_forward(2)
    z_forward(3)
    for cp in q_in + sib:
        cp.wait_recv()

    def block_prep(b, _):
        kq = b // 4
        kp = lax.rem(b, 4)
        gg, ii = peer(kp=-kp, kq=-kq)
        row = ids[pl.ds(gg * 8 + ii, 1), :]
        idi[b] = jnp.broadcast_to(row, (B, B)).T
        img[pl.ds(pl.multiple_of(b * B, B), B), :] = imgT[b].astype(f32).T.astype(bf16)
        return 0

    lax.fori_loop(0, 16, block_prep, 0)

    s2 = scale_ref[0] * LOG2E
    b2 = bias_ref[0] * LOG2E
    CH = 512

    def text_ids(j, s):
        gg, ii = mesh_id(x, y, lax.rem(z + j, 8), lax.rem(c + s, 2))
        return ids[pl.ds(gg * 8 + ii, 1), :]

    def core_copy(j):
        return remote(gt.at[j, 1], rcore.at[j], s_rs.at[j], r_rs.at[j], kc=1)

    def right_copy(t):
        return remote(gt.at[4 - t, 0], rright.at[t], s_rs.at[8 + t], r_rs.at[8 + t], kz=1)

    def left_copy(t):
        return remote(gt.at[4 + t, 0], rleft.at[t], s_rs.at[12 + t], r_rs.at[12 + t], kz=-1)

    def hand_on(t):
        core_copy(4 + t).wait_recv()
        gt[4 + t, 0] += rcore[4 + t]
        core_copy(3 - t).wait_recv()
        gt[3 - t, 0] += rcore[3 - t]

        @pl.when(t == 0)
        def _():
            right_copy(0).start()

        @pl.when(t > 0)
        def _():
            @pl.when(t > 1)
            def _():
                left_copy(t - 1).wait_recv()
                gt[4 + t, 0] += rleft[t - 1]
            left_copy(t).start()
            right_copy(t - 1).wait_recv()
            gt[4 - t, 0] += rright[t - 1]
            right_copy(t).start()

    def tile(t, _):
        ja = 4 + t
        jb = 3 - t
        tT = jnp.concatenate([txtT[ja, 0], txtT[ja, 1], txtT[jb, 0], txtT[jb, 1]], axis=1)
        idt = jnp.concatenate([text_ids(ja, 0), text_ids(ja, 1), text_ids(jb, 0), text_ids(jb, 1)], axis=1)

        def dots_of(ch):
            return jnp.dot(img[pl.ds(ch * CH, CH), :], tT, preferred_element_type=f32)

        def coef_of(ch, dots):
            ii = jnp.concatenate([idi[4 * ch + k] for k in range(4)], axis=0)
            match = jnp.concatenate([ii] * 4, axis=1) == idt
            loss, co = score(dots, match, s2, b2)
            part = (loss[:, :B] + loss[:, B:2 * B]) + (loss[:, 2 * B:3 * B] + loss[:, 3 * B:])
            lacc[pl.ds(ch * CH, CH), :] += part
            return co

        def grads_of(ch, co, acc):
            iT = jnp.concatenate([imgT[4 * ch + k] for k in range(4)], axis=1)
            g = jnp.dot(iT, co, preferred_element_type=f32)
            h = dg(tT, co, 1, 1)
            for k in range(4):
                gi[4 * ch + k, 0:D, :] += h[:, k * B:(k + 1) * B]
            return g if acc is None else acc + g

        nch = 4
        d = {0: dots_of(0)}
        co = {}
        acc = None
        for ch in range(nch + 1):
            if ch + 1 < nch:
                d[ch + 1] = dots_of(ch + 1)
            if ch < nch:
                co[ch] = coef_of(ch, d.pop(ch))
            if ch >= 1:
                acc = grads_of(ch - 1, co.pop(ch - 1), acc)
        gt[ja, 0] = acc[:, :B]
        gt[ja, 1] = acc[:, B:2 * B]
        gt[jb, 0] = acc[:, 2 * B:3 * B]
        gt[jb, 1] = acc[:, 3 * B:]
        core_copy(ja).start()
        core_copy(jb).start()

        @pl.when(t > 0)
        def _():
            hand_on(t - 1)
        return 0

    lax.fori_loop(0, 4, tile, 0)

    def r1_copy(k, j):
        i = (k - 1) * 4 + j
        return remote(gi.at[4 * k + j], r1.at[i], s_rs.at[16 + i], r_rs.at[16 + i], kq=-k)

    def r2_copy(k):
        return remote(gi.at[k], r2.at[k - 1], s_rs.at[28 + k], r_rs.at[28 + k], kp=-k)

    def loss_row(b, _):
        gi[b, D:GR, :] = jnp.broadcast_to(
            jnp.sum(lacc[pl.ds(pl.multiple_of(b * B, B), B), :].T, axis=0, keepdims=True), (8, B))
        return 0

    lax.fori_loop(0, 16, loss_row, 0)
    for j in (2, 1, 3, 0):
        for k in (2, 1, 3):
            r1_copy(k, j).start()

    hand_on(3)
    left_copy(3).wait_recv()
    right_copy(3).wait_recv()
    tg = ((gt[0, 0] + rleft[3]) + rright[3]) * scale_ref[0]
    pg = normalize_back(tg.T, txtu[...], invs[1][:, :1]).astype(bf16)
    txt_out[...] = dg(pg, head[...], 1, 1)
    part = HEAD_SCALE * dg(feat[...], pg, 0, 0)
    part = jnp.concatenate([part, jnp.zeros((D, 64), f32)], axis=1)
    for k in range(5):
        hp[72 * k:72 * (k + 1)] = part[:, k * B:(k + 1) * B].reshape(72, 8, B)
    hp[360:HT] = jnp.zeros((HT - 360, 8, B), f32)

    def ar(j, src, dst, **k):
        return remote(src, dst, s_ar.at[j], r_ar.at[j], **k)

    h0 = ar(0, hp.at[pl.ds((1 - c) * 192, 192)], hcore, kc=1)
    h0.start()

    def r1_sum(j):
        for k in (1, 2, 3):
            r1_copy(k, j).wait_recv()
            gi[j] += r1[(k - 1) * 4 + j]

    h0.wait()
    hcore[...] += hp[pl.ds(c * 192, 192)]
    hp_copies = []
    for k in (1, 2, 3):
        cp = ar(k, hcore.at[pl.ds(lax.rem(pp + k, 4) * 48, 48)], hP.at[k - 1], kp=k)
        cp.start()
        hp_copies.append(cp)
    for j in (2, 1, 3):
        r1_sum(j)
        r2_copy(j).start()
    r1_sum(0)
    for cp in hp_copies:
        cp.wait()
    hcore[pl.ds(pp * 48, 48)] += (hP[0] + hP[1]) + hP[2]
    hq_copies = []
    for k in (1, 2, 3):
        cp = ar(3 + k, hcore.at[pl.ds(pp * 48 + lax.rem(qq + k, 4) * 12, 12)], hQ.at[k - 1], kq=k)
        cp.start()
        hq_copies.append(cp)
    for k in (1, 2, 3):
        r2_copy(k).wait_recv()
    ig = (gi[0] + r2[0]) + (r2[1] + r2[2])
    loss_out[...] = ig[D:D + 1, :] / (256 * B)
    img_out[...] = normalize_back((ig[0:D, :] * scale_ref[0]).T, imgu[...], invs[0][:, :1])
    for cp in hq_copies:
        cp.wait()
    hz[z] = hcore[pl.ds(pp * 48 + qq * 12, 12)] + ((hQ[0] + hQ[1]) + hQ[2])
    hz_copies = []
    for k in range(1, 8):
        cp = ar(6 + k, hz.at[z], hz.at[z], kz=k)
        cp.start()
        hz_copies.append(cp)
    for cp in hz_copies:
        cp.wait()
    tot = hz[0]
    for k in range(1, 8):
        tot = tot + hz[k]
    base = c * 192 + pp * 48
    res[pl.ds(base + qq * 12, 12)] = tot
    cps = []
    for k in (1, 2, 3):
        sl = pl.ds(base + qq * 12, 12)
        cp = ar(13 + k, res.at[sl], res.at[sl], kq=k)
        cp.start()
        cps.append(cp)
    for cp in cps:
        cp.wait()
    cps = []
    for k in (1, 2, 3):
        sl = pl.ds(base, 48)
        cp = ar(16 + k, res.at[sl], res.at[sl], kp=k)
        cp.start()
        cps.append(cp)
    for cp in cps:
        cp.wait()
    sl = pl.ds(c * 192, 192)
    cp = ar(20, res.at[sl], res.at[sl], kc=1)
    cp.start()
    cp.wait()
    for k in range(5):
        w = min(B, D - k * B)
        head_out[:, k * B:k * B + w] = res[72 * k:72 * (k + 1)].reshape(D, B)[:, :w]

    for cp in started:
        cp.wait_send()
    for j in range(8):
        core_copy(j).wait_send()
    for t in range(4):
        right_copy(t).wait_send()
        if t:
            left_copy(t).wait_send()
    for j in range(4):
        for k in (1, 2, 3):
            r1_copy(k, j).wait_send()
    for k in (1, 2, 3):
        r2_copy(k).wait_send()


def shards(image_emb, text_feat, text_head, pair_ids, logit_scale, logit_bias):
    vm = pl.BlockSpec(memory_space=pltpu.VMEM)
    sm = pl.BlockSpec(memory_space=pltpu.SMEM)
    V = pltpu.VMEM
    ids = pair_ids.reshape(256, B).astype(f32)
    loss, img_g, txt_g, head_g = pl.pallas_call(
        kernel,
        in_specs=[sm, sm, vm, vm, vm, vm],
        out_specs=[vm, vm, vm, vm],
        out_shape=[
            jax.ShapeDtypeStruct((1, B), f32),
            jax.ShapeDtypeStruct((B, D), f32),
            jax.ShapeDtypeStruct((B, D), f32),
            jax.ShapeDtypeStruct((D, D), f32),
        ],
        scratch_shapes=[
            V((16, D, B), bf16), V((16 * B, D), bf16), V((8, 2, D, B), bf16), V((16, B, B), f32),
            V((16 * B, B), f32), V((16, GR, B), f32), V((8, 2, D, B), f32),
            V((B, D), f32), V((B, D), f32), V((2, B, B), f32),
            V((8, D, B), f32), V((4, D, B), f32), V((4, D, B), f32),
            V((12, GR, B), f32), V((3, GR, B), f32),
            V((HT, 8, B), f32), V((HT // 2, 8, B), f32), V((3, 48, 8, B), f32), V((3, 12, 8, B), f32),
            V((8, 12, 8, B), f32), V((HT, 8, B), f32),
            pltpu.SemaphoreType.DMA((32,)), pltpu.SemaphoreType.DMA((32,)),
            pltpu.SemaphoreType.DMA((32,)), pltpu.SemaphoreType.DMA((32,)),
            pltpu.SemaphoreType.DMA((24,)), pltpu.SemaphoreType.DMA((24,)),
        ],
        compiler_params=pltpu.CompilerParams(
            collective_id=0, has_side_effects=True, vmem_limit_bytes=60 * 2**20),
        name="pair_loss",
    )(logit_scale, logit_bias, image_emb, text_feat, text_head, ids)
    return loss.reshape(B), img_g, txt_g, head_g


def solution(mesh):
    return jax.shard_map(
        shards,
        mesh=mesh,
        in_specs=(P(("group", "inner"), None), P(("group", "inner"), None), P(), P(), P(), P()),
        out_specs=(
            P(("group", "inner")),
            P(("group", "inner"), None),
            P(("group", "inner"), None),
            P(),
        ),
        check_vma=False,
    )
```

time: 882 us -> 151 us (0.17)
  waiting for transfers between devices: 495 us -> 0 us
  matrix products: 289 us -> 0 us
  Pallas kernels: 0 us -> 137 us
  local copies, waits for them, and re-layouts: 31.6 us -> 10.8 us
  starting transfers between devices: 20.2 us -> 0 us
  blocking collectives: 16.7 us -> 0 us
  between operations: 14.5 us -> 1.93 us
    dot_general x99 -> x0, matrix products: 289 us -> none  [the longest x32 119 us: score_tile(): lax.dot_general(text_block, images, (((1,), (1,)), ((), ())), preferred_e...]
    psum x1 -> x0, waiting for transfers between devices: 236 us -> none  [shards(): head_grad = lax.psum(head_part, ('group', 'inner'))]
    pallas_call x0 -> x1, Pallas kernels: none -> 137 us  [shards(): pl.pallas_call(kernel, in_specs=[sm, sm, vm, vm, vm, vm], out_specs=[vm,...]
    ppermute x64 -> x0, waiting for transfers between devices: 123 us -> none  [passed_along(): lax.ppermute(value, axis, [(i, (i + by) % peers) for i in range(peers)])]
    reduce_scatter x1 -> x0, waiting for transfers between devices: 81.6 us -> none  [shards(): lax.psum_scatter(image_total, 'inner', scatter_dimension=0, tiled=True)]
    all_gather x1 -> x0, waiting for transfers between devices: 52.5 us -> none  [shards(): lax.all_gather(img_unit_f.astype(jnp.bfloat16), 'inner', axis=0, tiled=True)]
    dynamic_slice x17 -> x0, local copies, waits for them, and re-layouts: 23.2 us -> none  [the longest x16 22 us: score_tile(): block_ids = lax.dynamic_slice_in_dim(pair_ids, start, row_count)]
    ppermute x64 -> x0, starting transfers between devices: 20.1 us -> none  [passed_along(): lax.ppermute(value, axis, [(i, (i + by) % peers) for i in range(peers)])]
  transfers between devices with their start and end apart: 67 -> 0, of which waited for: 32 -> 0; matrix products, arithmetic and copies ran while one was open for 36% -> 0% of each run, Pallas kernels for 0% -> 0%
where the time goes in v1:
time: 151 us
  Pallas kernels  137 us (91%)
  local copies, waits for them, and re-layouts  10.8 us (7%)
  between operations  1.93 us (1%)
  other arithmetic  1.57 us (1%)
    pallas_call x1, Pallas kernels, shards(): pl.pallas_call(kernel, in_specs=[sm, sm, vm, vm, vm, vm], out_specs=[vm,...  137 us
    unnamed x6, local copies, waits for them, and re-layouts  10.8 us

profile of v1, /device:TPU:1, one launch (start us, length us, event | category | flops | bytes accessed | tf_op | source)
XLA Modules:
  0.0 151.0 jit_solution(18255902797707917067)
XLA Ops:
  1.9 1.6 %convert_bitcast_fusion.ids = f32[256,128]{1,0:T(8,128)} fusion(s32[32768]{0:T(1024)} %param.9), kind=kLoop, calls=%fused_computation | loop fusion | flops 32768 | bytes 262144 | tf_op jit(solution)/shard_map/convert_element_type | solution.py:367
  3.5 1.7 %copy.10.emb = bf16[128,576]{1,0:T(8,128)(2,1)} copy(bf16[128,576]{0,1:T(8,128)(2,1)} %param.6) | data formatting | bytes 294912 | tf_op args[0]
  5.2 1.7 %copy.11.feat = bf16[128,576]{1,0:T(8,128)(2,1)} copy(bf16[128,576]{0,1:T(8,128)(2,1)} %param.7) | data formatting | bytes 294912 | tf_op args[1]
  6.9 136.8 %pair_loss.1 = (f32[1,128]{1,0:T(1,128)}, f32[128,576]{1,0:T(8,128)}, f32[128,576]{1,0:T(8,128)}, f32[576,576]{1,0:T(8,128)}) custom-call(f32[1]{0:T(128)S(6)} %copy.16.scale_ref, f32[1]{0:T(128)S(6)} %copy.17.bias_ref, bf16[128,576]{1,0:T(8,128)(2,1)} %copy.10.emb, bf16[128,576]{1,0:T(8,128)(2,1)} %copy.11.feat, bf16[576,576]{1,0:T(8,128)(2,1)} %head.1, ...), custom_call_target="tpu_custom_call" | custom-call | tf_op jit(solution)/shard_map/pair_loss/pallas_call | solution.py:368
  143.7 1.8 %copy.12 = f32[128,576]{0,1:T(8,128)} copy(f32[128,576]{1,0:T(8,128)} %get-tuple-element.13) | data formatting | bytes 589824
  145.5 1.8 %copy.13 = f32[128,576]{0,1:T(8,128)} copy(f32[128,576]{1,0:T(8,128)} %get-tuple-element.14) | data formatting | bytes 589824
  147.4 1.1 copy.18
  148.5 2.6 %copy.19 = f32[576,576]{1,0:T(8,128)} copy(f32[576,576]{1,0:T(8,128)} %get-tuple-element.23) | data formatting | bytes 2654208

commit v2 on v1

v2 whole, which is shorter than its diff:
```python
import jax
import jax.numpy as jnp
from jax import lax
from jax.experimental import pallas as pl
from jax.experimental.pallas import tpu as pltpu
from jax.sharding import PartitionSpec as P

HEAD_SCALE = 16.0
LOG2E = 1.4426950408889634
D = 576
B = 128
PR = 384
QR = 96
XR = 16
f32 = jnp.float32
bf16 = jnp.bfloat16


def dg(a, b, ca, cb):
    return lax.dot_general(a, b, (((ca,), (cb,)), ((), ())), preferred_element_type=f32)


def coords():
    g = lax.axis_index("group")
    i = lax.axis_index("inner")
    return lax.rem(i, 2) * 2 + g // 16, i // 2, lax.rem(g // 2, 8), lax.rem(g, 2)


def mesh_id(x, y, z, c):
    return (lax.rem(x, 2) * 8 + z) * 2 + c, y * 2 + x // 2


def peer(kp=0, kq=0, kz=0, kc=0):
    x, y, z, c = coords()
    dx = jnp.where(c == 0, kp, kq)
    dy = jnp.where(c == 0, kq, kp)
    return mesh_id(
        lax.rem(x + dx + 4, 4), lax.rem(y + dy + 4, 4), lax.rem(z + kz + 8, 8), lax.rem(c + kc, 2)
    )


def remote(src, dst, ss, rs, **k):
    return pltpu.make_async_remote_copy(
        src_ref=src, dst_ref=dst, send_sem=ss, recv_sem=rs,
        device_id=peer(**k), device_id_type=pl.DeviceIdType.MESH,
    )


def score(dots, match, s2, b2):
    z = dots * s2 + b2
    m = jnp.where(match, -z, z)
    u = jnp.exp2(m)
    w = 1.0 + u
    r = 1.0 / w
    sg = u * r
    loss = jnp.log(w) + (u - (w - 1.0)) * r
    return loss, jnp.where(match, -sg, sg).astype(bf16)


def coded(v):
    top = jnp.maximum(jnp.max(jnp.abs(v), axis=0, keepdims=True), 1e-30)
    return jnp.round(v * (32766.0 / top)).astype(jnp.int32).astype(jnp.int16), top * (1.0 / 32766.0)


def decoded(q, scale):
    return q.astype(jnp.int32).astype(f32) * scale


def packed(v):
    top = jnp.maximum(jnp.max(jnp.abs(v), axis=0, keepdims=True), 1e-30)
    k = jnp.ceil(jnp.log2(top) + 0.001) - 15.0
    q = jnp.clip(jnp.round(v * jnp.exp2(-k)), -32767.0, 32767.0)
    q = jnp.concatenate([q, jnp.broadcast_to(k, (XR, B))], axis=0)
    return q.astype(jnp.int32).astype(jnp.int16)


def unpacked(q):
    n = q.shape[0] - XR
    f = q.astype(jnp.int32).astype(f32)
    return f[:n] * jnp.exp2(f[n:n + 1])


def kernel(scale_ref, bias_ref, embT, featT, head, ids,
           misc, res,
           imgT, img, txtT, idi, lacc, cbuf, gi, gt, imgu, txtu, invs, fsib, pgs,
           rcore, rright, rleft, q1, q1s, c1, c1s, q2, q2s, c2, c2s, hp, hPs, hP, hQs, hQ, hz,
           s_ag, r_ag, s_rs, r_rs, s_ar, r_ar):
    x, y, z, c = coords()
    pp = jnp.where(c == 0, x, y)
    qq = jnp.where(c == 0, y, x)
    bar = pltpu.get_barrier_semaphore()
    partners = ([dict(kp=k) for k in (1, 2, 3)] + [dict(kq=k) for k in (1, 2, 3)]
                + [dict(kz=k) for k in range(1, 8)] + [dict(kc=1)])
    for k in partners:
        pl.semaphore_signal(bar, inc=1, device_id=peer(**k), device_id_type=pl.DeviceIdType.MESH)

    e = embT[...].astype(f32)
    inv = lax.rsqrt(jnp.sum(e * e, axis=0, keepdims=True) + 1e-06)
    imgu[...] = e * inv
    invs[0:1, :] = inv
    imgT[0] = (e * inv).astype(bf16)
    projT = dg(featT[...], head[...], 0, 0).T
    vinv = lax.rsqrt(jnp.sum(projT * projT, axis=0, keepdims=True) + 1e-06)
    txtu[...] = projT * vinv
    invs[8:9, :] = vinv
    txtT[0, 0] = (projT * vinv).astype(bf16)
    pl.semaphore_wait(bar, len(partners))

    n = [0]
    started = []

    def go(src, dst, **k):
        j = n[0]
        n[0] += 1
        cp = remote(src, dst, s_ag.at[j], r_ag.at[j], **k)
        cp.start()
        started.append(cp)
        return cp

    H = D // 2
    half = [pl.ds(0, H), pl.ds(H, H)]
    quick = {}

    def slot(h, a, b):
        return 4 * b + a if h == 0 else 4 * a + b

    def first(h, k):
        return dict(kp=k) if h == 0 else dict(kq=k)

    def second(h, k):
        return dict(kq=k) if h == 0 else dict(kp=k)

    def hop(h, src, dst, axis, k):
        s = slot(h, *src)
        d = slot(h, *dst)
        quick[h, dst] = go(imgT.at[s, half[h]], imgT.at[d, half[h]], **axis(h, k))

    def spread(h, a):
        hop(h, (a, 0), (a, 1), second, 1)
        hop(h, (a, 0), (a, 3), second, -1)

    def arrived(h, a, b):
        quick.pop((h, (a, b))).wait_recv()

    for h in (0, 1):
        hop(h, (0, 0), (1, 0), first, 1)
        hop(h, (0, 0), (3, 0), first, -1)
    z_right = {}
    z_left = {}
    for h in (0, 1):
        z_right[0, h] = go(txtT.at[0, 0, half[h]], txtT.at[7, 0, half[h]], kz=1)
        z_left[0, h] = go(txtT.at[0, 0, half[h]], txtT.at[1, 0, half[h]], kz=-1)
    spread(0, 0)
    spread(1, 0)
    sib = [go(txtT.at[0, 0], txtT.at[0, 1], kc=1), go(featT, fsib, kc=1)]

    lacc[...] = jnp.zeros_like(lacc)

    def id_prep(b, _):
        gg, ii = peer(kp=-lax.rem(b, 4), kq=-(b // 4))
        row = ids[pl.ds(gg * 8 + ii, 1), :].astype(f32)
        idi[b] = jnp.broadcast_to(row, (B, B)).T
        return 0

    lax.fori_loop(0, 16, id_prep, 0)

    def img_prep(b):
        img[pl.ds(pl.multiple_of(b * B, B), B), :] = imgT[b].astype(f32).T.astype(bf16)

    def z_forward(s):
        a = 7 - s
        b = 1 + s
        for h in (0, 1):
            if (s, h) in z_right:
                z_right[s, h].wait_recv()
                if s < 2 or (s == 2 and h == 0):
                    z_right[s + 1, h] = go(txtT.at[a, 0, half[h]], txtT.at[a - 1, 0, half[h]], kz=1)
            if (s, h) in z_left:
                z_left[s, h].wait_recv()
                if s < 2 or (s == 2 and h == 1):
                    z_left[s + 1, h] = go(txtT.at[b, 0, half[h]], txtT.at[b + 1, 0, half[h]], kz=-1)
        sib.append(go(txtT.at[a, 0], txtT.at[a, 1], kc=1))
        if s < 3:
            sib.append(go(txtT.at[b, 0], txtT.at[b, 1], kc=1))

    def far(h, a):
        if h == 0:
            arrived(h, a, 1)
            hop(h, (a, 1), (a, 2), second, 1)
        else:
            arrived(h, a, 3)
            hop(h, (a, 3), (a, 2), second, -1)

    arrived(0, 1, 0)
    hop(0, (1, 0), (2, 0), first, 1)
    spread(0, 1)
    arrived(1, 3, 0)
    hop(1, (3, 0), (2, 0), first, -1)
    spread(1, 3)
    arrived(0, 3, 0)
    spread(0, 3)
    arrived(1, 1, 0)
    spread(1, 1)
    z_forward(0)
    far(0, 0)
    far(1, 0)
    for h in (0, 1):
        arrived(h, 2, 0)
        spread(h, 2)
    z_forward(1)
    far(0, 1)
    far(1, 3)
    far(0, 3)
    far(1, 1)
    z_forward(2)
    far(0, 2)
    far(1, 2)
    near = [(h, d) for (h, d) in quick if 2 not in d]
    for h, d in near:
        arrived(h, *d)

    def near_prep(r, _):
        kp = lax.rem(r, 3)
        kq = r // 3
        img_prep(4 * (kq + kq // 2) + kp + kp // 2)
        return 0

    lax.fori_loop(0, 9, near_prep, 0)
    z_forward(3)
    for h, d in list(quick):
        arrived(h, *d)

    def far_prep(r, _):
        img_prep(8 + r)
        return 0

    def far_prep2(r, _):
        img_prep(4 * (r + r // 2) + 2)
        return 0

    lax.fori_loop(0, 4, far_prep, 0)
    lax.fori_loop(0, 3, far_prep2, 0)
    for cp in sib:
        cp.wait_recv()

    s2 = scale_ref[0] * LOG2E
    b2 = bias_ref[0] * LOG2E
    CH = 512

    def text_ids(j, s):
        gg, ii = mesh_id(x, y, lax.rem(z + j, 8), lax.rem(c + s, 2))
        return ids[pl.ds(gg * 8 + ii, 1), :].astype(f32)

    def core_copy(j):
        return remote(gt.at[j, 1], rcore.at[j], s_rs.at[j], r_rs.at[j], kc=1)

    def hslice(h):
        return pl.ds(h * H, H)

    def right_copy(t, h):
        i = 8 + 2 * t + h
        return remote(gt.at[4 - t, 0, hslice(h)], rright.at[t, hslice(h)], s_rs.at[i], r_rs.at[i], kz=1)

    def left_copy(t, h):
        i = 16 + 2 * t + h
        return remote(gt.at[4 + t, 0, hslice(h)], rleft.at[t, hslice(h)], s_rs.at[i], r_rs.at[i], kz=-1)

    def take_right(t, h):
        right_copy(t - 1, h).wait_recv()
        gt[4 - t, 0, hslice(h)] += rright[t - 1, hslice(h)]

    def take_left(t, h):
        left_copy(t - 1, h).wait_recv()
        gt[4 + t, 0, hslice(h)] += rleft[t - 1, hslice(h)]

    def cores(t):
        core_copy(4 + t).wait_recv()
        gt[4 + t, 0] += rcore[4 + t]
        core_copy(3 - t).wait_recv()
        gt[3 - t, 0] += rcore[3 - t]

    def between(t):
        @pl.when(t == 1)
        def _():
            cores(0)
            right_copy(0, 0).start()
            left_copy(0, 1).start()

        @pl.when(t == 2)
        def _():
            cores(1)
            right_copy(1, 1).start()
            left_copy(1, 0).start()

        @pl.when(t == 3)
        def _():
            cores(2)
            take_right(1, 0)
            right_copy(1, 0).start()
            take_left(1, 1)
            left_copy(1, 1).start()

    def chain(t):
        for h in (0, 1):
            take_right(t, 1 - h)
            right_copy(t, 1 - h).start()
            take_left(t, h)
            left_copy(t, h).start()

    def tile(t, _):
        ja = 4 + t
        jb = 3 - t
        tT = jnp.concatenate([txtT[ja, 0], txtT[ja, 1], txtT[jb, 0], txtT[jb, 1]], axis=1)
        idt = jnp.concatenate([text_ids(ja, 0), text_ids(ja, 1), text_ids(jb, 0), text_ids(jb, 1)], axis=1)

        def dots_of(ch):
            return jnp.dot(img[pl.ds(ch * CH, CH), :], tT, preferred_element_type=f32)

        def coef_of(ch, dots):
            ii = jnp.concatenate([idi[4 * ch + k] for k in range(4)], axis=0)
            match = jnp.concatenate([ii] * 4, axis=1) == idt
            loss, co = score(dots, match, s2, b2)
            part = (loss[:, :B] + loss[:, B:2 * B]) + (loss[:, 2 * B:3 * B] + loss[:, 3 * B:])
            lacc[pl.ds(ch * CH, CH), :] += part
            return co

        def grads_of(ch, co, acc):
            iT = jnp.concatenate([imgT[4 * ch + k] for k in range(4)], axis=1)
            cbuf[t, ch] = co
            g = jnp.dot(iT, co, preferred_element_type=f32)
            return g if acc is None else acc + g

        nch = 4
        d = {0: dots_of(0)}
        co = {}
        acc = None
        for ch in range(nch + 1):
            if ch + 1 < nch:
                d[ch + 1] = dots_of(ch + 1)
            if ch < nch:
                co[ch] = coef_of(ch, d.pop(ch))
            if ch == 0:
                between(t)
            if ch >= 1:
                acc = grads_of(ch - 1, co.pop(ch - 1), acc)
        gt[ja, 0] = acc[:, :B]
        gt[ja, 1] = acc[:, B:2 * B]
        core_copy(ja).start()
        gt[jb, 0] = acc[:, 2 * B:3 * B]
        gt[jb, 1] = acc[:, 3 * B:]
        core_copy(jb).start()
        return 0

    lax.fori_loop(0, 4, tile, 0)

    def r1_copy(k, j):
        i = (k - 1) * 4 + j
        return remote(c1.at[i], q1.at[i], s_rs.at[24 + i], r_rs.at[24 + i], kq=-k)

    def r1s_copy(k):
        i = 36 + k
        return remote(c1s.at[k - 1], q1s.at[k - 1], s_rs.at[i], r_rs.at[i], kq=-k)

    def r2_copy(k):
        i = 40 + k
        return remote(c2.at[k - 1], q2.at[k - 1], s_rs.at[i], r_rs.at[i], kp=-k)

    def r2s_copy(k):
        i = 44 + k
        return remote(c2s.at[k - 1], q2s.at[k - 1], s_rs.at[i], r_rs.at[i], kp=-k)

    def loss_of(b):
        return jnp.sum(lacc[pl.ds(pl.multiple_of(b * B, B), B), :].T, axis=0, keepdims=True)

    def encode(k):
        def one(j, _):
            q, sc = coded(gi[4 * k + j])
            c1[(k - 1) * 4 + j] = q
            c1s[k - 1, j, 0:1, :] = sc
            c1s[k - 1, j, 1:2, :] = loss_of(4 * k + j)
            r1_copy(k, j).start()
            return 0
        lax.fori_loop(0, 4, one, 0)
        r1s_copy(k).start()

    def image_part(ch):
        at = [b for t in range(4) for b in ((4 + t, 0), (4 + t, 1), (3 - t, 0), (3 - t, 1))]
        tT = jnp.concatenate([txtT[j, s] for j, s in at], axis=1)
        co = jnp.concatenate([cbuf[t, ch] for t in range(4)], axis=1)
        h = dg(tT, co, 1, 1)
        for k in range(4):
            gi[4 * ch + k] = h[:, k * B:(k + 1) * B]

    image_part(2)
    cores(3)
    encode(2)
    chain(2)
    image_part(1)
    encode(1)
    image_part(3)
    encode(3)
    chain(3)
    image_part(0)

    for h in (0, 1):
        left_copy(3, h).wait_recv()
        right_copy(3, h).wait_recv()
    tg = ((gt[0, 0] + rleft[3]) + rright[3]) * scale_ref[0]
    tu = txtu[...]
    pgT = (invs[8:9, :] * (tg - tu * jnp.sum(tu * tg, axis=0, keepdims=True))).astype(bf16)
    pgs[0] = pgT

    def ar(j, src, dst, **k):
        return remote(src, dst, s_ar.at[j], r_ar.at[j], **k)

    cp = ar(0, pgs.at[0], pgs.at[1], kc=1)
    cp.start()
    misc[D:2 * D, :] = jnp.dot(head[...], pgT, preferred_element_type=f32)
    cp.wait()
    rows = pl.ds(pl.multiple_of(c * H, 32), H)
    f2 = jnp.concatenate([featT[rows, :], fsib[rows, :]], axis=1)
    p2 = jnp.concatenate([pgs[0], pgs[1]], axis=1)
    part = HEAD_SCALE * dg(f2, p2, 1, 1)
    for k in range(4):
        hp[H * k:H * (k + 1), :] = part[:, k * B:(k + 1) * B]
    hp[4 * H:5 * H, :] = jnp.concatenate([part[:, 4 * B:], jnp.zeros((H, 64), f32)], axis=1)
    hp[5 * H:4 * PR, :] = jnp.zeros((4 * PR - 5 * H, B), f32)

    def hp_rows(p, q, n):
        return pl.ds(pl.multiple_of(p * PR + q * QR, 32), n)

    cps = []
    for k in (2, 1, 3):
        hPs[k - 1] = packed(hp[hp_rows(lax.rem(pp + k, 4), 0, PR), :])
        cp = ar(k, hPs.at[k - 1], hP.at[k - 1], kp=k)
        cp.start()
        cps.append(cp)

    for k in (1, 3, 2):
        r1s_copy(k).wait_recv()

    def r1_sum(j):
        v = gi[j]
        ls = loss_of(j)
        for k in (1, 3, 2):
            r1_copy(k, j).wait_recv()
            v = v + decoded(q1[(k - 1) * 4 + j], q1s[k - 1, j, 0:1, :])
            ls = ls + q1s[k - 1, j, 1:2, :]
        return v, ls

    for j in (2, 1, 3):
        v, ls = r1_sum(j)
        q, sc = coded(v)
        c2[j - 1] = q
        c2s[j - 1, 0:1, :] = sc
        c2s[j - 1, 1:2, :] = ls
        r2_copy(j).start()
        r2s_copy(j).start()
    for cp in cps:
        cp.wait()
    hp[hp_rows(pp, 0, PR), :] += (unpacked(hP[0]) + unpacked(hP[1])) + unpacked(hP[2])
    cps = []
    for k in (2, 1, 3):
        hQs[k - 1] = packed(hp[hp_rows(pp, lax.rem(qq + k, 4), QR), :])
        cp = ar(3 + k, hQs.at[k - 1], hQ.at[k - 1], kq=k)
        cp.start()
        cps.append(cp)
    v0, ls0 = r1_sum(0)
    for cp in cps:
        cp.wait()
    tot = hp[hp_rows(pp, qq, QR), :] + ((unpacked(hQ[0]) + unpacked(hQ[1])) + unpacked(hQ[2]))
    hz[z] = packed(tot)
    cps = []
    for k in (4, 3, 5, 2, 6, 1, 7):
        cp = ar(6 + k, hz.at[z], hz.at[z], kz=k)
        cp.start()
        cps.append(cp)

    for k in (1, 3, 2):
        r2s_copy(k).wait_recv()
        r2_copy(k).wait_recv()
        v0 = v0 + decoded(q2[k - 1], q2s[k - 1, 0:1, :])
        ls0 = ls0 + q2s[k - 1, 1:2, :]
    ig = v0 * scale_ref[0]
    iu = imgu[...]
    misc[0:D, :] = invs[0:1, :] * (ig - iu * jnp.sum(iu * ig, axis=0, keepdims=True))
    misc[2 * D:2 * D + 8, :] = jnp.broadcast_to(ls0 / (256 * B), (8, B))

    for cp in cps:
        cp.wait()
    tot = unpacked(hz[0])
    for k in range(1, 8):
        tot = tot + unpacked(hz[k])
    base = c * 16 + pp * 4
    res[base + qq] = packed(tot)
    cps = []
    for k in (2, 1, 3):
        cp = ar(20 + k, res.at[base + qq], res.at[base + qq], kq=k)
        cp.start()
        cps.append(cp)
    for cp in cps:
        cp.wait()
    own = pl.ds(base, 4)
    pcs = {}
    for k in (2, 1, 3):
        pcs[k] = ar(23 + k, res.at[own], res.at[own], kp=k)
        pcs[k].start()
    ccs = [ar(27, res.at[own], res.at[own], kc=1)]
    ccs[0].start()
    for k in (1, 3, 2):
        pcs[k].wait()
        sl = pl.ds(c * 16 + lax.rem(pp + 4 - k, 4) * 4, 4)
        cp = ar(27 + k, res.at[sl], res.at[sl], kc=1)
        cp.start()
        ccs.append(cp)
    for cp in ccs:
        cp.wait()

    for cp in started:
        cp.wait_send()
    for j in range(8):
        core_copy(j).wait_send()
    for t in range(4):
        for h in (0, 1):
            if t or h == 0:
                right_copy(t, h).wait_send()
            if t or h == 1:
                left_copy(t, h).wait_send()
    for k in (1, 2, 3):
        for j in range(4):
            r1_copy(k, j).wait_send()
        r1s_copy(k).wait_send()
        r2_copy(k).wait_send()
        r2s_copy(k).wait_send()


def write_out(misc, res, loss, img, txt, head):
    loss[...] = misc[2 * D:2 * D + 1, :]
    img[...] = misc[0:D, :]
    txt[...] = misc[D:2 * D, :]
    H = D // 2
    for c in range(2):
        half = jnp.concatenate([unpacked(res[16 * c + n]) for n in range(16)], axis=0)
        for k in range(5):
            w = min(B, D - k * B)
            head[c * H:(c + 1) * H, k * B:k * B + w] = half[k * H:(k + 1) * H, :w]


def shards(image_emb, text_feat, text_head, pair_ids, logit_scale, logit_bias):
    vm = pl.BlockSpec(memory_space=pltpu.VMEM)
    sm = pl.BlockSpec(memory_space=pltpu.SMEM)
    V = pltpu.VMEM
    i16 = jnp.int16
    dma = pltpu.SemaphoreType.DMA
    misc, res = pl.pallas_call(
        kernel,
        in_specs=[sm, sm, vm, vm, vm, vm],
        out_specs=[vm, vm],
        out_shape=[
            jax.ShapeDtypeStruct((2 * D + 8, B), f32),
            jax.ShapeDtypeStruct((32, QR + XR, B), i16),
        ],
        scratch_shapes=[
            V((16, D, B), bf16), V((16 * B, D), bf16), V((8, 2, D, B), bf16), V((16, B, B), f32),
            V((16 * B, B), f32), V((4, 4, 512, 512), bf16), V((16, D, B), f32), V((8, 2, D, B), f32),
            V((D, B), f32), V((D, B), f32), V((16, B), f32), V((D, B), bf16), V((2, D, B), bf16),
            V((8, D, B), f32), V((4, D, B), f32), V((4, D, B), f32),
            V((12, D, B), i16), V((3, 4, 8, B), f32), V((12, D, B), i16), V((3, 4, 8, B), f32),
            V((3, D, B), i16), V((3, 8, B), f32), V((3, D, B), i16), V((3, 8, B), f32),
            V((4 * PR, B), f32), V((3, PR + XR, B), i16), V((3, PR + XR, B), i16),
            V((3, QR + XR, B), i16), V((3, QR + XR, B), i16), V((8, QR + XR, B), i16),
            dma((56,)), dma((56,)), dma((48,)), dma((48,)), dma((32,)), dma((32,)),
        ],
        compiler_params=pltpu.CompilerParams(
            collective_id=0, has_side_effects=True, vmem_limit_bytes=60 * 2**20),
        name="pair_loss",
    )(logit_scale, logit_bias, image_emb.T, text_feat.T, text_head, pair_ids.reshape(256, B))
    loss, img_g, txt_g, head_g = pl.pallas_call(
        write_out,
        in_specs=[vm, vm],
        out_specs=[vm, vm, vm, vm],
        out_shape=[
            jax.ShapeDtypeStruct((1, B), f32),
            jax.ShapeDtypeStruct((D, B), f32),
            jax.ShapeDtypeStruct((D, B), f32),
            jax.ShapeDtypeStruct((D, D), f32),
        ],
        name="write_out",
    )(misc, res)
    return loss.reshape(B), img_g.T, txt_g.T, head_g


def solution(mesh):
    return jax.shard_map(
        shards,
        mesh=mesh,
        in_specs=(P(("group", "inner"), None), P(("group", "inner"), None), P(), P(), P(), P()),
        out_specs=(
            P(("group", "inner")),
            P(("group", "inner"), None),
            P(("group", "inner"), None),
            P(),
        ),
        check_vma=False,
    )
```

time: 151 us -> 105 us (0.70)
  Pallas kernels: 137 us -> 103 us
  local copies, waits for them, and re-layouts: 10.8 us -> 0 us
  other arithmetic: 1.57 us -> 0 us
    pallas_call x1, Pallas kernels: 137 us -> 101 us  [shards(): pl.pallas_call(kernel, in_specs=[sm, sm, vm, vm, vm, vm], out_specs=[vm,...]
    unnamed x6 -> x0, local copies, waits for them, and re-layouts: 10.8 us -> none
    pallas_call x0 -> x1, Pallas kernels: none -> 2.69 us  [shards(): pl.pallas_call(write_out, in_specs=[vm, vm], out_specs=[vm, vm, vm, vm],...]
    convert_element_type x1 -> x0, other arithmetic: 1.57 us -> none  [shards(): ids = pair_ids.reshape(256, B).astype(f32)]
where the time goes in v2:
time: 105 us
  Pallas kernels  103 us (98%)
  between operations  1.93 us (2%)
    pallas_call x1, Pallas kernels, shards(): pl.pallas_call(kernel, in_specs=[sm, sm, vm, vm, vm, vm], out_specs=[vm,...  101 us
    pallas_call x1, Pallas kernels, shards(): pl.pallas_call(write_out, in_specs=[vm, vm], out_specs=[vm, vm, vm, vm],...  2.69 us

profile of v2, /device:TPU:1, one launch (start us, length us, event | category | flops | bytes accessed | tf_op | source)
XLA Modules:
  0.0 105.3 jit_solution(2346415215864148371)
XLA Ops:
  1.9 100.7 %pair_loss.1 = (f32[1160,128]{1,0:T(8,128)}, s16[32,112,128]{2,1,0:T(8,128)(2,1)}) custom-call(f32[1]{0:T(128)S(6)} %copy.10.scale_ref, f32[1]{0:T(128)S(6)} %copy.11.bias_ref, bf16[576,128]{1,0:T(8,128)(2,1)} %bitcast.6, bf16[576,128]{1,0:T(8,128)(2,1)} %bitcast.7, bf16[576,576]{1,0:T(8,128)(2,1)} %head.1, s32[256,128]{1,0:T(8,128)} %bitcast.8), custom_call_target="tpu_custom_call" | custom-call | tf_op jit(solution)/shard_map/pair_loss/pallas_call | solution.py:555
  102.6 2.7 %write_out.1 = (f32[1,128]{1,0:T(1,128)}, f32[576,128]{1,0:T(8,128)}, f32[576,128]{1,0:T(8,128)}, f32[576,576]{1,0:T(8,128)}) custom-call(f32[1160,128]{1,0:T(8,128)} %get-tuple-element.10.misc, s16[32,112,128]{2,1,0:T(8,128)(2,1)} %get-tuple-element.11.res), custom_call_target="tpu_custom_call" | custom-call | tf_op jit(solution)/shard_map/write_out/pallas_call | solution.py:578

commit v3 on v2

--- a/solution.py
+++ b/solution.py
@@ -57,21 +57,22 @@
     return loss, jnp.where(match, -sg, sg).astype(bf16)
 
 
-def coded(v):
-    top = jnp.maximum(jnp.max(jnp.abs(v), axis=0, keepdims=True), 1e-30)
-    return jnp.round(v * (32766.0 / top)).astype(jnp.int32).astype(jnp.int16), top * (1.0 / 32766.0)
-
-
-def decoded(q, scale):
-    return q.astype(jnp.int32).astype(f32) * scale
-
-
-def packed(v):
-    top = jnp.maximum(jnp.max(jnp.abs(v), axis=0, keepdims=True), 1e-30)
-    k = jnp.ceil(jnp.log2(top) + 0.001) - 15.0
+def power(top):
+    return jnp.ceil(jnp.log2(jnp.maximum(top, 1e-30)) + 0.001) - 15.0
+
+
+def packed(v, a=None):
+    k = power(jnp.max(jnp.abs(v), axis=0, keepdims=True))
     q = jnp.clip(jnp.round(v * jnp.exp2(-k)), -32767.0, 32767.0)
-    q = jnp.concatenate([q, jnp.broadcast_to(k, (XR, B))], axis=0)
-    return q.astype(jnp.int32).astype(jnp.int16)
+    if a is None:
+        rest = jnp.broadcast_to(k, (XR, B))
+    else:
+        ka = power(jnp.abs(a))
+        hi = jnp.clip(jnp.round(a * jnp.exp2(-ka)), -32767.0, 32767.0)
+        lo = jnp.clip(jnp.round((a * jnp.exp2(-ka) - hi) * 32768.0), -32767.0, 32767.0)
+        i = lax.broadcasted_iota(jnp.int32, (XR, B), 0)
+        rest = jnp.where(i == 0, k, jnp.where(i == 1, ka, jnp.where(i == 2, hi, lo)))
+    return jnp.concatenate([q, rest], axis=0).astype(jnp.int32).astype(jnp.int16)
 
 
 def unpacked(q):
@@ -80,10 +81,16 @@
     return f[:n] * jnp.exp2(f[n:n + 1])
 
 
+def row_of(q):
+    n = q.shape[0] - XR
+    f = q[n:].astype(jnp.int32).astype(f32)
+    return (f[2:3] + f[3:4] * (1.0 / 32768.0)) * jnp.exp2(f[1:2])
+
+
 def kernel(scale_ref, bias_ref, embT, featT, head, ids,
            misc, res,
            imgT, img, txtT, idi, lacc, cbuf, gi, gt, imgu, txtu, invs, fsib, pgs,
-           rcore, rright, rleft, q1, q1s, c1, c1s, q2, q2s, c2, c2s, hp, hPs, hP, hQs, hQ, hz,
+           rcore, along, sright, sleft, rright, rleft, sa, ra, sb, rb, slo, rlo, sc, rc, sm, rm, hp, hPs, hP, hQs, hQ, hz,
            s_ag, r_ag, s_rs, r_rs, s_ar, r_ar):
     x, y, z, c = coords()
     pp = jnp.where(c == 0, x, y)
@@ -163,6 +170,34 @@
         return 0
 
     lax.fori_loop(0, 16, id_prep, 0)
+
+    s2 = scale_ref[0] * LOG2E
+    b2 = bias_ref[0] * LOG2E
+    CH = 512
+
+    def text_ids(j, s):
+        gg, ii = mesh_id(x, y, lax.rem(z + j, 8), lax.rem(c + s, 2))
+        return ids[pl.ds(gg * 8 + ii, 1), :].astype(f32)
+
+    def text_tile(t):
+        at = [(4 + t, 0), (4 + t, 1), (3 - t, 0), (3 - t, 1)]
+        return (jnp.concatenate([txtT[j, s] for j, s in at], axis=1),
+                jnp.concatenate([text_ids(j, s) for j, s in at], axis=1))
+
+    def dots_of(ch, tT):
+        return jnp.dot(img[pl.ds(ch * CH, CH), :], tT, preferred_element_type=f32)
+
+    def coef_of(ch, dots, idt):
+        ii = jnp.concatenate([idi[4 * ch + k] for k in range(4)], axis=0)
+        match = jnp.concatenate([ii] * 4, axis=1) == idt
+        loss, co = score(dots, match, s2, b2)
+        part = (loss[:, :B] + loss[:, B:2 * B]) + (loss[:, 2 * B:3 * B] + loss[:, 3 * B:])
+        lacc[pl.ds(ch * CH, CH), :] += part
+        return co
+
+    def score_early(t):
+        tT, idt = text_tile(t)
+        cbuf[t, 0] = coef_of(0, dots_of(0, tT), idt)
 
     def img_prep(b):
         img[pl.ds(pl.multiple_of(b * B, B), B), :] = imgT[b].astype(f32).T.astype(bf16)
@@ -212,9 +247,23 @@
     far(1, 3)
     far(0, 3)
     far(1, 1)
+    arrived(1, 0, 1)
+    arrived(1, 0, 2)
+
+    def own_prep(r, _):
+        img_prep(r)
+        return 0
+
+    lax.fori_loop(0, 4, own_prep, 0)
+    sib[0].wait_recv()
+    sib[2].wait_recv()
+    score_early(3)
     z_forward(2)
     far(0, 2)
     far(1, 2)
+    sib[3].wait_recv()
+    sib[4].wait_recv()
+    score_early(2)
     near = [(h, d) for (h, d) in quick if 2 not in d]
     for h, d in near:
         arrived(h, *d)
@@ -225,7 +274,10 @@
         img_prep(4 * (kq + kq // 2) + kp + kp // 2)
         return 0
 
-    lax.fori_loop(0, 9, near_prep, 0)
+    lax.fori_loop(3, 9, near_prep, 0)
+    sib[5].wait_recv()
+    sib[6].wait_recv()
+    score_early(1)
     z_forward(3)
     for h, d in list(quick):
         arrived(h, *d)
@@ -239,17 +291,10 @@
         return 0
 
     lax.fori_loop(0, 4, far_prep, 0)
-    lax.fori_loop(0, 3, far_prep2, 0)
-    for cp in sib:
-        cp.wait_recv()
-
-    s2 = scale_ref[0] * LOG2E
-    b2 = bias_ref[0] * LOG2E
-    CH = 512
-
-    def text_ids(j, s):
-        gg, ii = mesh_id(x, y, lax.rem(z + j, 8), lax.rem(c + s, 2))
-        return ids[pl.ds(gg * 8 + ii, 1), :].astype(f32)
+    lax.fori_loop(1, 3, far_prep2, 0)
+    for n in (1, 7, 8):
+        sib[n].wait_recv()
+    score_early(0)
 
     def core_copy(j):
         return remote(gt.at[j, 1], rcore.at[j], s_rs.at[j], r_rs.at[j], kc=1)
@@ -259,89 +304,111 @@
 
     def right_copy(t, h):
         i = 8 + 2 * t + h
-        return remote(gt.at[4 - t, 0, hslice(h)], rright.at[t, hslice(h)], s_rs.at[i], r_rs.at[i], kz=1)
+        return remote(sright.at[t, h], rright.at[t, h], s_rs.at[i], r_rs.at[i], kz=1)
 
     def left_copy(t, h):
         i = 16 + 2 * t + h
-        return remote(gt.at[4 + t, 0, hslice(h)], rleft.at[t, hslice(h)], s_rs.at[i], r_rs.at[i], kz=-1)
+        return remote(sleft.at[t, h], rleft.at[t, h], s_rs.at[i], r_rs.at[i], kz=-1)
+
+    def along_row(j):
+        return along[pl.ds(j, 1), :]
+
+    def send(buf, copy, t, j, h):
+        buf[t, h] = packed(gt[j, 0, hslice(h)], along_row(j) if h == 0 else None)
+        copy(t, h).start()
+
+    def send_right(t, h):
+        send(sright, right_copy, t, 4 - t, h)
+
+    def send_left(t, h):
+        send(sleft, left_copy, t, 4 + t, h)
+
+    def take(buf, t, j, h):
+        got = buf[t - 1, h]
+        gt[j, 0, hslice(h)] += unpacked(got)
+        if h == 0:
+            along[pl.ds(j, 1), :] = along_row(j) + row_of(got)
 
     def take_right(t, h):
         right_copy(t - 1, h).wait_recv()
-        gt[4 - t, 0, hslice(h)] += rright[t - 1, hslice(h)]
+        take(rright, t, 4 - t, h)
 
     def take_left(t, h):
         left_copy(t - 1, h).wait_recv()
-        gt[4 + t, 0, hslice(h)] += rleft[t - 1, hslice(h)]
+        take(rleft, t, 4 + t, h)
 
     def cores(t):
-        core_copy(4 + t).wait_recv()
-        gt[4 + t, 0] += rcore[4 + t]
-        core_copy(3 - t).wait_recv()
-        gt[3 - t, 0] += rcore[3 - t]
-
-    def between(t):
-        @pl.when(t == 1)
-        def _():
-            cores(0)
-            right_copy(0, 0).start()
-            left_copy(0, 1).start()
-
-        @pl.when(t == 2)
-        def _():
-            cores(1)
-            right_copy(1, 1).start()
-            left_copy(1, 0).start()
-
-        @pl.when(t == 3)
-        def _():
-            cores(2)
-            take_right(1, 0)
-            right_copy(1, 0).start()
-            take_left(1, 1)
-            left_copy(1, 1).start()
+        for j in (4 + t, 3 - t):
+            core_copy(j).wait_recv()
+            g = gt[j, 0] + rcore[j]
+            uj = txtT[j, 0].astype(f32)
+            a = (jnp.sum(uj * g, axis=0, keepdims=True)
+                 / jnp.maximum(jnp.sum(uj * uj, axis=0, keepdims=True), 1e-30))
+            along[pl.ds(j, 1), :] = a
+            gt[j, 0] = g - a * uj
 
     def chain(t):
         for h in (0, 1):
             take_right(t, 1 - h)
-            right_copy(t, 1 - h).start()
+            send_right(t, 1 - h)
             take_left(t, h)
-            left_copy(t, h).start()
+            send_left(t, h)
+
+    def between(t, late):
+        if not late:
+            @pl.when(t == 1)
+            def _():
+                cores(0)
+                send_right(0, 0)
+                send_left(0, 1)
+
+            @pl.when(t == 2)
+            def _():
+                cores(1)
+                send_right(1, 1)
+                send_left(1, 0)
+
+            @pl.when(t == 3)
+            def _():
+                cores(2)
+        else:
+            @pl.when(t == 2)
+            def _():
+                take_right(1, 0)
+                send_right(1, 0)
+                take_left(1, 1)
+                send_left(1, 1)
+
+            @pl.when(t == 3)
+            def _():
+                chain(2)
 
     def tile(t, _):
         ja = 4 + t
         jb = 3 - t
-        tT = jnp.concatenate([txtT[ja, 0], txtT[ja, 1], txtT[jb, 0], txtT[jb, 1]], axis=1)
-        idt = jnp.concatenate([text_ids(ja, 0), text_ids(ja, 1), text_ids(jb, 0), text_ids(jb, 1)], axis=1)
-
-        def dots_of(ch):
-            return jnp.dot(img[pl.ds(ch * CH, CH), :], tT, preferred_element_type=f32)
-
-        def coef_of(ch, dots):
-            ii = jnp.concatenate([idi[4 * ch + k] for k in range(4)], axis=0)
-            match = jnp.concatenate([ii] * 4, axis=1) == idt
-            loss, co = score(dots, match, s2, b2)
-            part = (loss[:, :B] + loss[:, B:2 * B]) + (loss[:, 2 * B:3 * B] + loss[:, 3 * B:])
-            lacc[pl.ds(ch * CH, CH), :] += part
-            return co
+        tT, idt = text_tile(t)
 
         def grads_of(ch, co, acc):
             iT = jnp.concatenate([imgT[4 * ch + k] for k in range(4)], axis=1)
-            cbuf[t, ch] = co
+            if ch:
+                cbuf[t, ch] = co
             g = jnp.dot(iT, co, preferred_element_type=f32)
             return g if acc is None else acc + g
 
         nch = 4
-        d = {0: dots_of(0)}
+        d = {1: dots_of(1, tT)}
+        acc = grads_of(0, cbuf[t, 0], None)
         co = {}
-        acc = None
-        for ch in range(nch + 1):
+        for ch in range(1, nch + 1):
             if ch + 1 < nch:
-                d[ch + 1] = dots_of(ch + 1)
+                d[ch + 1] = dots_of(ch + 1, tT)
             if ch < nch:
-                co[ch] = coef_of(ch, d.pop(ch))
-            if ch == 0:
-                between(t)
-            if ch >= 1:
+                co[ch] = coef_of(ch, d.pop(ch), idt)
+            if ch == 1:
+                between(t, False)
+            if ch == 3:
+                between(t, True)
+            if ch >= 2:
                 acc = grads_of(ch - 1, co.pop(ch - 1), acc)
         gt[ja, 0] = acc[:, :B]
         gt[ja, 1] = acc[:, B:2 * B]
@@ -353,35 +420,54 @@
 
     lax.fori_loop(0, 4, tile, 0)
 
-    def r1_copy(k, j):
-        i = (k - 1) * 4 + j
-        return remote(c1.at[i], q1.at[i], s_rs.at[24 + i], r_rs.at[24 + i], kq=-k)
-
-    def r1s_copy(k):
-        i = 36 + k
-        return remote(c1s.at[k - 1], q1s.at[k - 1], s_rs.at[i], r_rs.at[i], kq=-k)
-
-    def r2_copy(k):
-        i = 40 + k
-        return remote(c2.at[k - 1], q2.at[k - 1], s_rs.at[i], r_rs.at[i], kp=-k)
-
-    def r2s_copy(k):
-        i = 44 + k
-        return remote(c2s.at[k - 1], q2s.at[k - 1], s_rs.at[i], r_rs.at[i], kp=-k)
+    def ra_copy(h, j):
+        i = 24 + h * 4 + j
+        return remote(sa.at[h, j], ra.at[h, j], s_rs.at[i], r_rs.at[i], kq=1 if h else -1)
+
+    def rb_copy(h, j):
+        i = 32 + h * 4 + j
+        return remote(sb.at[h, j], rb.at[h, j], s_rs.at[i], r_rs.at[i], kq=1 if h else -1)
+
+    def rl_copy(k):
+        i = 39 + k
+        return remote(slo.at[k - 1], rlo.at[k - 1], s_rs.at[i], r_rs.at[i], kq=-k)
+
+    def rc_copy(k):
+        i = 42 + k
+        return remote(sc.at[k - 1], rc.at[k - 1], s_rs.at[i], r_rs.at[i], kp=-k)
+
+    def rm_copy(k):
+        i = 45 + k
+        return remote(sm.at[k - 1], rm.at[k - 1], s_rs.at[i], r_rs.at[i], kp=-k)
 
     def loss_of(b):
         return jnp.sum(lacc[pl.ds(pl.multiple_of(b * B, B), B), :].T, axis=0, keepdims=True)
 
-    def encode(k):
+    def send_far():
         def one(j, _):
-            q, sc = coded(gi[4 * k + j])
-            c1[(k - 1) * 4 + j] = q
-            c1s[k - 1, j, 0:1, :] = sc
-            c1s[k - 1, j, 1:2, :] = loss_of(4 * k + j)
-            r1_copy(k, j).start()
+            for h in (0, 1):
+                sa[h, j] = packed(gi[8 + j, hslice(h)])
+                ra_copy(h, j).start()
             return 0
         lax.fori_loop(0, 4, one, 0)
-        r1s_copy(k).start()
+
+    def send_near(h):
+        def one(j, _):
+            b = 12 + j if h else 4 + j
+            ra_copy(h, j).wait_recv()
+            gi[b, hslice(h)] += unpacked(ra[h, j])
+            sb[h, j] = packed(gi[b])
+            rb_copy(h, j).start()
+            return 0
+        lax.fori_loop(0, 4, one, 0)
+
+    def send_losses():
+        for k in (1, 2, 3):
+            def one(j, _):
+                slo[k - 1, pl.ds(j, 1), :] = loss_of(4 * k + j)
+                return 0
+            lax.fori_loop(0, 4, one, 0)
+            rl_copy(k).start()
 
     def image_part(ch):
         at = [b for t in range(4) for b in ((4 + t, 0), (4 + t, 1), (3 - t, 0), (3 - t, 1))]
@@ -392,20 +478,20 @@
             gi[4 * ch + k] = h[:, k * B:(k + 1) * B]
 
     image_part(2)
+    send_far()
+    image_part(1)
+    image_part(3)
     cores(3)
-    encode(2)
-    chain(2)
-    image_part(1)
-    encode(1)
-    image_part(3)
-    encode(3)
     chain(3)
-    image_part(0)
+    send_near(0)
+    send_near(1)
 
     for h in (0, 1):
         left_copy(3, h).wait_recv()
         right_copy(3, h).wait_recv()
-    tg = ((gt[0, 0] + rleft[3]) + rright[3]) * scale_ref[0]
+    tg = jnp.concatenate([(gt[0, 0, hslice(h)] + unpacked(rleft[3, h])) + unpacked(rright[3, h]) for h in (0, 1)], axis=0)
+    a = (along_row(0) + row_of(rleft[3, 0])) + row_of(rright[3, 0])
+    tg = (tg + a * txtT[0, 0].astype(f32)) * scale_ref[0]
     tu = txtu[...]
     pgT = (invs[8:9, :] * (tg - tu * jnp.sum(tu * tg, axis=0, keepdims=True))).astype(bf16)
     pgs[0] = pgT
@@ -436,26 +522,8 @@
         cp.start()
         cps.append(cp)
 
-    for k in (1, 3, 2):
-        r1s_copy(k).wait_recv()
-
-    def r1_sum(j):
-        v = gi[j]
-        ls = loss_of(j)
-        for k in (1, 3, 2):
-            r1_copy(k, j).wait_recv()
-            v = v + decoded(q1[(k - 1) * 4 + j], q1s[k - 1, j, 0:1, :])
-            ls = ls + q1s[k - 1, j, 1:2, :]
-        return v, ls
-
-    for j in (2, 1, 3):
-        v, ls = r1_sum(j)
-        q, sc = coded(v)
-        c2[j - 1] = q
-        c2s[j - 1, 0:1, :] = sc
-        c2s[j - 1, 1:2, :] = ls
-        r2_copy(j).start()
-        r2s_copy(j).start()
+    image_part(0)
+    send_losses()
     for cp in cps:
         cp.wait()
     hp[hp_rows(pp, 0, PR), :] += (unpacked(hP[0]) + unpacked(hP[1])) + unpacked(hP[2])
@@ -465,7 +533,7 @@
         cp = ar(3 + k, hQs.at[k - 1], hQ.at[k - 1], kq=k)
         cp.start()
         cps.append(cp)
-    v0, ls0 = r1_sum(0)
+
     for cp in cps:
         cp.wait()
     tot = hp[hp_rows(pp, qq, QR), :] + ((unpacked(hQ[0]) + unpacked(hQ[1])) + unpacked(hQ[2]))
@@ -476,16 +544,24 @@
         cp.start()
         cps.append(cp)
 
-    for k in (1, 3, 2):
-        r2s_copy(k).wait_recv()
-        r2_copy(k).wait_recv()
-        v0 = v0 + decoded(q2[k - 1], q2s[k - 1, 0:1, :])
-        ls0 = ls0 + q2s[k - 1, 1:2, :]
-    ig = v0 * scale_ref[0]
-    iu = imgu[...]
-    misc[0:D, :] = invs[0:1, :] * (ig - iu * jnp.sum(iu * ig, axis=0, keepdims=True))
-    misc[2 * D:2 * D + 8, :] = jnp.broadcast_to(ls0 / (256 * B), (8, B))
-
+    for k in (1, 2, 3):
+        rl_copy(k).wait_recv()
+
+    def r1_sum(j):
+        v = gi[j]
+        for h in (0, 1):
+            rb_copy(h, j).wait_recv()
+            v = v + unpacked(rb[h, j])
+        ls = (loss_of(j) + rlo[0, j:j + 1, :]) + (rlo[1, j:j + 1, :] + rlo[2, j:j + 1, :])
+        return v, ls
+
+    for j in (2, 1, 3):
+        v, ls = r1_sum(j)
+        sc[j - 1] = packed(v)
+        rc_copy(j).start()
+        sm[j - 1] = jnp.broadcast_to(ls, (8, B))
+        rm_copy(j).start()
+    v0, ls0 = r1_sum(0)
     for cp in cps:
         cp.wait()
     tot = unpacked(hz[0])
@@ -508,6 +584,15 @@
     ccs = [ar(27, res.at[own], res.at[own], kc=1)]
     ccs[0].start()
     for k in (1, 3, 2):
+        rm_copy(k).wait_recv()
+        rc_copy(k).wait_recv()
+        v0 = v0 + unpacked(rc[k - 1])
+        ls0 = ls0 + rm[k - 1, 0:1, :]
+    ig = v0 * scale_ref[0]
+    iu = imgu[...]
+    misc[0:D, :] = invs[0:1, :] * (ig - iu * jnp.sum(iu * ig, axis=0, keepdims=True))
+    misc[2 * D:2 * D + 8, :] = jnp.broadcast_to(ls0 / (256 * B), (8, B))
+    for k in (1, 3, 2):
         pcs[k].wait()
         sl = pl.ds(c * 16 + lax.rem(pp + 4 - k, 4) * 4, 4)
         cp = ar(27 + k, res.at[sl], res.at[sl], kc=1)
@@ -526,12 +611,14 @@
                 right_copy(t, h).wait_send()
             if t or h == 1:
                 left_copy(t, h).wait_send()
+    for h in (0, 1):
+        for j in range(4):
+            ra_copy(h, j).wait_send()
+            rb_copy(h, j).wait_send()
     for k in (1, 2, 3):
-        for j in range(4):
-            r1_copy(k, j).wait_send()
-        r1s_copy(k).wait_send()
-        r2_copy(k).wait_send()
-        r2s_copy(k).wait_send()
+        rl_copy(k).wait_send()
+        rc_copy(k).wait_send()
+        rm_copy(k).wait_send()
 
 
 def write_out(misc, res, loss, img, txt, head):
@@ -564,12 +651,18 @@
             V((16, D, B), bf16), V((16 * B, D), bf16), V((8, 2, D, B), bf16), V((16, B, B), f32),
             V((16 * B, B), f32), V((4, 4, 512, 512), bf16), V((16, D, B), f32), V((8, 2, D, B), f32),
             V((D, B), f32), V((D, B), f32), V((16, B), f32), V((D, B), bf16), V((2, D, B), bf16),
-            V((8, D, B), f32), V((4, D, B), f32), V((4, D, B), f32),
-            V((12, D, B), i16), V((3, 4, 8, B), f32), V((12, D, B), i16), V((3, 4, 8, B), f32),
-            V((3, D, B), i16), V((3, 8, B), f32), V((3, D, B), i16), V((3, 8, B), f32),
+            V((8, D, B), f32), V((8, B), f32),
+            V((4, 2, D // 2 + XR, B), i16),
+            V((4, 2, D // 2 + XR, B), i16),
+            V((4, 2, D // 2 + XR, B), i16),
+            V((4, 2, D // 2 + XR, B), i16),
+            V((2, 4, D // 2 + XR, B), i16), V((2, 4, D // 2 + XR, B), i16),
+            V((2, 4, D + XR, B), i16), V((2, 4, D + XR, B), i16),
+            V((3, 8, B), f32), V((3, 8, B), f32),
+            V((3, D + XR, B), i16), V((3, D + XR, B), i16), V((3, 8, B), f32), V((3, 8, B), f32),
             V((4 * PR, B), f32), V((3, PR + XR, B), i16), V((3, PR + XR, B), i16),
             V((3, QR + XR, B), i16), V((3, QR + XR, B), i16), V((8, QR + XR, B), i16),
-            dma((56,)), dma((56,)), dma((48,)), dma((48,)), dma((32,)), dma((32,)),
+            dma((56,)), dma((56,)), dma((52,)), dma((52,)), dma((32,)), dma((32,)),
         ],
         compiler_params=pltpu.CompilerParams(
             collective_id=0, has_side_effects=True, vmem_limit_bytes=60 * 2**20),

time: 105 us -> 103 us (0.981)
  Pallas kernels: 103 us -> 101 us
    pallas_call x1, Pallas kernels: 101 us -> 98.2 us  [shards(): pl.pallas_call(kernel, in_specs=[sm, sm, vm, vm, vm, vm], out_specs=[vm,...]
where the time goes in v3:
time: 103 us
  Pallas kernels  101 us (98%)
  between operations  1.93 us (2%)
    pallas_call x1, Pallas kernels, shards(): pl.pallas_call(kernel, in_specs=[sm, sm, vm, vm, vm, vm], out_specs=[vm,...  98.2 us
    pallas_call x1, Pallas kernels, shards(): pl.pallas_call(write_out, in_specs=[vm, vm], out_specs=[vm, vm, vm, vm],...  2.69 us

profile of v3, /device:TPU:1, one launch (start us, length us, event | category | flops | bytes accessed | tf_op | source)
XLA Modules:
  0.0 102.8 jit_solution(11710564846924697275)
XLA Ops:
  1.9 98.2 %pair_loss.1 = (f32[1160,128]{1,0:T(8,128)}, s16[32,112,128]{2,1,0:T(8,128)(2,1)}) custom-call(f32[1]{0:T(128)S(6)} %copy.10.scale_ref, f32[1]{0:T(128)S(6)} %copy.11.bias_ref, bf16[576,128]{1,0:T(8,128)(2,1)} %bitcast.6, bf16[576,128]{1,0:T(8,128)(2,1)} %bitcast.7, bf16[576,576]{1,0:T(8,128)(2,1)} %head.1, s32[256,128]{1,0:T(8,128)} %bitcast.8), custom_call_target="tpu_custom_call" | custom-call | tf_op jit(solution)/shard_map/pair_loss/pallas_call | solution.py:642
  100.1 2.7 %write_out.1 = (f32[1,128]{1,0:T(1,128)}, f32[576,128]{1,0:T(8,128)}, f32[576,128]{1,0:T(8,128)}, f32[576,576]{1,0:T(8,128)}) custom-call(f32[1160,128]{1,0:T(8,128)} %get-tuple-element.10.misc, s16[32,112,128]{2,1,0:T(8,128)(2,1)} %get-tuple-element.11.res), custom_call_target="tpu_custom_call" | custom-call | tf_op jit(solution)/shard_map/write_out/pallas_call | solution.py:671

commit v4 on v3

--- a/solution.py
+++ b/solution.py
@@ -569,18 +569,24 @@
         tot = tot + unpacked(hz[k])
     base = c * 16 + pp * 4
     res[base + qq] = packed(tot)
-    cps = []
+    q_back = {}
     for k in (2, 1, 3):
-        cp = ar(20 + k, res.at[base + qq], res.at[base + qq], kq=k)
-        cp.start()
-        cps.append(cp)
-    for cp in cps:
-        cp.wait()
+        q_back[k] = ar(20 + k, res.at[base + qq], res.at[base + qq], kq=k)
+        q_back[k].start()
+    pcs = {1: [], 2: [], 3: []}
+
+    def p_back(n):
+        at = base + lax.rem(qq + 4 - n, 4)
+        for k in (2, 1, 3):
+            cp = ar(28 + 4 * k + n, res.at[at], res.at[at], kp=k)
+            cp.start()
+            pcs[k].append(cp)
+
+    p_back(0)
+    for n in (1, 3, 2):
+        q_back[n].wait()
+        p_back(n)
     own = pl.ds(base, 4)
-    pcs = {}
-    for k in (2, 1, 3):
-        pcs[k] = ar(23 + k, res.at[own], res.at[own], kp=k)
-        pcs[k].start()
     ccs = [ar(27, res.at[own], res.at[own], kc=1)]
     ccs[0].start()
     for k in (1, 3, 2):
@@ -593,7 +599,8 @@
     misc[0:D, :] = invs[0:1, :] * (ig - iu * jnp.sum(iu * ig, axis=0, keepdims=True))
     misc[2 * D:2 * D + 8, :] = jnp.broadcast_to(ls0 / (256 * B), (8, B))
     for k in (1, 3, 2):
-        pcs[k].wait()
+        for cp in pcs[k]:
+            cp.wait()
         sl = pl.ds(c * 16 + lax.rem(pp + 4 - k, 4) * 4, 4)
         cp = ar(27 + k, res.at[sl], res.at[sl], kc=1)
         cp.start()
@@ -662,7 +669,7 @@
             V((3, D + XR, B), i16), V((3, D + XR, B), i16), V((3, 8, B), f32), V((3, 8, B), f32),
             V((4 * PR, B), f32), V((3, PR + XR, B), i16), V((3, PR + XR, B), i16),
             V((3, QR + XR, B), i16), V((3, QR + XR, B), i16), V((8, QR + XR, B), i16),
-            dma((56,)), dma((56,)), dma((52,)), dma((52,)), dma((32,)), dma((32,)),
+            dma((56,)), dma((56,)), dma((52,)), dma((52,)), dma((48,)), dma((48,)),
         ],
         compiler_params=pltpu.CompilerParams(
             collective_id=0, has_side_effects=True, vmem_limit_bytes=60 * 2**20),

time: 103 us -> 103 us (level)
  no operation moved by 1% of the time
where the time goes in v4:
time: 103 us
  Pallas kernels  101 us (98%)
  between operations  1.93 us (2%)
    pallas_call x1, Pallas kernels, shards(): pl.pallas_call(kernel, in_specs=[sm, sm, vm, vm, vm, vm], out_specs=[vm,...  97.9 us
    pallas_call x1, Pallas kernels, shards(): pl.pallas_call(write_out, in_specs=[vm, vm], out_specs=[vm, vm, vm, vm],...  2.69 us

profile of v4, /device:TPU:1, one launch (start us, length us, event | category | flops | bytes accessed | tf_op | source)
XLA Modules:
  0.0 102.6 jit_solution(8184400049716716715)
XLA Ops:
  1.9 97.9 %pair_loss.1 = (f32[1160,128]{1,0:T(8,128)}, s16[32,112,128]{2,1,0:T(8,128)(2,1)}) custom-call(f32[1]{0:T(128)S(6)} %copy.10.scale_ref, f32[1]{0:T(128)S(6)} %copy.11.bias_ref, bf16[576,128]{1,0:T(8,128)(2,1)} %bitcast.6, bf16[576,128]{1,0:T(8,128)(2,1)} %bitcast.7, bf16[576,576]{1,0:T(8,128)(2,1)} %head.1, s32[256,128]{1,0:T(8,128)} %bitcast.8), custom_call_target="tpu_custom_call" | custom-call | tf_op jit(solution)/shard_map/pair_loss/pallas_call | solution.py:649
  99.9 2.7 %write_out.1 = (f32[1,128]{1,0:T(1,128)}, f32[576,128]{1,0:T(8,128)}, f32[576,128]{1,0:T(8,128)}, f32[576,576]{1,0:T(8,128)}) custom-call(f32[1160,128]{1,0:T(8,128)} %get-tuple-element.10.misc, s16[32,112,128]{2,1,0:T(8,128)(2,1)} %get-tuple-element.11.res), custom_call_target="tpu_custom_call" | custom-call | tf_op jit(solution)/shard_map/write_out/pallas_call | solution.py:678
